TPU v7x, 512 devices: a whole 4x8x8 slice. The times are simulated.
512 devices in a mesh: tm: 64 (over x, z, core), row: 8 (over y).
Axes of the slice: x: 4, y: 8, z: 8, core: 2. Of those that a mesh axis runs over, the one named last changes fastest.
Arguments:
- depth_tokens: bfloat16 [512, 8, 16, 768], P('tm', 'row'), may hold values from -6 to 6
- mixer_weight: bfloat16 [768, 800], replicated, may hold values from -0.21875 to 0.21875
- gate_weight: bfloat16 [768, 780], replicated, may hold values from -0.21875 to 0.21875
- conv_kernel: float32 [3, 3, 800], replicated, may hold values from -2 to 2
- conv_bias: float32 [800], replicated, may hold values from -3 to 3
- step_bias: float32 [12], replicated, may hold values from -1 to 1
- decay_rate: float32 [12], replicated, may hold values from 0 to 1, as said below
- skip_gain: float32 [12], replicated, may hold values from 0.5 to 1.5
- norm_gain: float32 [768], replicated, may hold values from 0.1 to 1.9
- out_weight: bfloat16 [768, 768], replicated, may hold values from -0.21875 to 0.21875
Outputs:
- refined: bfloat16 [512, 8, 16, 768], P('tm', 'row')
Inputs may be any that keep to these rules, and one draw needn't show every extreme that they name: `decay_rate`: one positive rate per head.
All inputs are finite; a program needn't handle non-finite values.
Results may differ from a plain program's by a relative error of at most 0.0064.
Values may be sent and summed in bfloat16 or wider, within the bound.
A program may use at most 128 MiB of HBM per device.

v0:
```python
import jax
import jax.numpy as jnp
from jax import lax
from jax.sharding import PartitionSpec as P

D = 768
HEADS = 12
HEAD_DIM = 64
NSTATE = 16
GW = 16
INNER = 768
CONV_CH = 800


def extended(block, sides, width):
    for axis, dim in sides:
        count = lax.axis_size(axis)
        forward = [(i, i + 1) for i in range(count - 1)]
        backward = [(target, source) for source, target in forward]
        low = lax.ppermute(
            lax.slice_in_dim(block, block.shape[dim] - width, None, axis=dim), axis, forward
        )
        high = lax.ppermute(lax.slice_in_dim(block, 0, width, axis=dim), axis, backward)
        block = jnp.concatenate([low, block, high], axis=dim)
    return block


def carried_in(part, axis, combine, identity):
    place = lax.axis_index(axis)
    gathered = jax.tree.map(lambda a: lax.all_gather(a, axis), part)
    state = jax.tree.map(lambda a, e: jnp.zeros_like(a) + jnp.asarray(e, a.dtype), part, identity)

    def one(step, state):
        return combine(
            state, jax.tree.map(lambda a: lax.dynamic_index_in_dim(a, step, 0, False), gathered)
        )

    return lax.fori_loop(0, place, one, state)


def combine_blocks(earlier, following):
    fade = following[0]
    carried = (
        earlier[1].reshape(earlier[1].shape[0], NSTATE, HEADS, HEAD_DIM) * fade[:, None, :, None]
    )
    return (earlier[0] * fade, carried.reshape(following[1].shape) + following[1])


def per_device(
    depth_tokens,
    mixer_weight,
    gate_weight,
    conv_kernel,
    conv_bias,
    step_bias,
    decay_rate,
    skip_gain,
    norm_gain,
    out_weight,
):
    frames = depth_tokens.shape[0]
    grid_rows = depth_tokens.shape[1]
    cell_count = grid_rows * GW
    flat_tokens = depth_tokens.reshape(-1, D)
    gate_step = jnp.dot(flat_tokens, gate_weight, preferred_element_type=jnp.float32).astype(
        jnp.bfloat16
    )
    conv_input = jnp.dot(flat_tokens, mixer_weight, preferred_element_type=jnp.float32).astype(
        jnp.bfloat16
    )
    conv_input = conv_input.reshape(frames, grid_rows, GW, CONV_CH)
    conv_window = extended(conv_input, (("row", 1),), 1)
    padded = jnp.pad(conv_window.astype(jnp.float32), ((0, 0), (0, 0), (1, 1), (0, 0)))
    summed = jnp.zeros((frames, grid_rows, GW, CONV_CH), jnp.float32) + conv_bias
    for row_shift in range(3):
        for col_shift in range(3):
            summed = (
                summed
                + conv_kernel[row_shift, col_shift]
                * padded[:, row_shift : row_shift + grid_rows, col_shift : col_shift + GW]
            )
    activated = jax.nn.silu(summed).reshape(frames, cell_count, CONV_CH)
    values = activated[..., :INNER].reshape(frames, cell_count, HEADS, HEAD_DIM)
    write_keys = activated[..., INNER : INNER + NSTATE]
    read_keys = activated[..., INNER + NSTATE :]
    gate_branch = gate_step[:, :INNER].astype(jnp.float32)
    step_size = jax.nn.softplus(gate_step[:, INNER:].astype(jnp.float32) + step_bias).reshape(
        frames, cell_count, HEADS
    )
    log_decay = -step_size * decay_rate
    running_decay = jnp.cumsum(log_decay, axis=0)
    span_decay = running_decay[-1]
    scaled_values = (jnp.exp(span_decay[None] - running_decay) * step_size)[..., None] * values
    end_state = jnp.einsum(
        "scn,schp->cnhp", write_keys, scaled_values, precision=lax.Precision.HIGHEST
    )
    identity = (
        jnp.ones((cell_count, HEADS), jnp.float32),
        jnp.zeros((cell_count, NSTATE, INNER), jnp.float32),
    )
    through_decay, incoming = carried_in(
        (jnp.exp(span_decay), end_state.reshape(cell_count, NSTATE, INNER)),
        "tm",
        combine_blocks,
        identity,
    )
    incoming = incoming.reshape(cell_count, NSTATE, HEADS, HEAD_DIM)

    def advance(carry_state, inputs):
        decay_now, step_now, value_now, write_now, read_now = inputs
        carry_state = (
            decay_now[:, None, :, None] * carry_state
            + (step_now[:, :, None] * value_now)[:, None] * write_now[:, :, None, None]
        )
        result = (
            jnp.einsum("cn,cnhp->chp", read_now, carry_state, precision=lax.Precision.HIGHEST)
            + skip_gain[:, None] * value_now
        )
        return (carry_state, result)

    final_state, output = lax.scan(
        advance, incoming, (jnp.exp(log_decay), step_size, values, write_keys, read_keys)
    )
    gated_out = output.reshape(-1, INNER) * jax.nn.silu(gate_branch)
    rms_scale = lax.rsqrt(jnp.mean(gated_out * gated_out, axis=-1, keepdims=True) + 1e-05)
    normed = (gated_out * rms_scale * norm_gain).astype(jnp.bfloat16)
    refined = flat_tokens.astype(jnp.float32) + jnp.dot(
        normed, out_weight, preferred_element_type=jnp.float32
    )
    return refined.astype(jnp.bfloat16).reshape(depth_tokens.shape)


def solution(mesh):
    placed = (P("tm", "row", None, None), P(), P(), P(), P(), P(), P(), P(), P(), P())
    return jax.shard_map(
        per_device,
        mesh=mesh,
        in_specs=placed,
        out_specs=P("tm", "row", None, None),
        check_vma=False,
    )
```

profile of v0, /device:TPU:455, one launch (start us, length us, event | category | flops | bytes accessed | tf_op | source)
XLA Modules:
  0.0 381.3 jit_solution(13413337569495677315)
XLA Ops:
  10.8 4.0 %collective-permute-start = (bf16[8,1,16,800]{3,0,2,1:T(8,128)(2,1)S(1)}, bf16[8,1,16,800]{3,0,2,1:T(8,128)(2,1)S(1)}, u32[]{:S(2)}, u32[]{:S(2)}) collective-permute-start(bf16[8,1,16,800]{3,0,2,1:T(8,128)(2,1)S(1)} %copy.40), channel_id=1, source_target_pairs={{0,1},{1,2},{2,3},{3,4},{4,5},{5,6},{6,7},{8,9},{9,10},{10,11},{11... | collective-permute-start | bytes 614408 | tf_op jit(solution)/shard_map/ppermute | solution.py:20
  16.3 1.5 collective-permute-done.1
  20.0 1.7 fusion.6
  23.7 49.5 %all_gather.7 = f32[64,16,12]{2,1,0:T(8,128)S(1)} all-gather(f32[1,16,12]{2,1,0:T(8,128)S(1)} %get-tuple-element.169), channel_id=1, replica_groups=mesh['tm'=64,'row'=8] {'tm'}, dimensions={0}, use_global_device_ids=true | all-gather | bytes 49920 | tf_op jit(solution)/shard_map/all_gather | solution.py:30
  74.3 142.1 %all-gather.2.cloned.1.call-done = f32[64,16,16,768]{3,2,1,0:T(8,128)} async-done(((f32[1,16,16,768]{3,2,1,0:T(8,128)}), f32[64,16,16,768]{3,2,1,0:T(8,128)}) %all-gather.2.cloned.1.call-update) | async-done | bytes 50331664 | tf_op jit(solution)/shard_map/all_gather | solution.py:30
  216.4 109.0 %while.24 = (s32[]{:T(128)}, f32[16,16,768]{2,1,0:T(8,128)S(1)}, s32[]{:T(128)}, f32[64,16,12]{2,1,0:T(8,128)S(1)}, f32[64,16,16,768]{3,2,1,0:T(8,128)}, /*index=5*/s32[]{:T(128)}, s32[]{:T(128)}, s32[]{:T(128)}) while((s32[]{:T(128)}, f32[16,16,768]{2,1,0:T(8,128)S(1)}, s32[]{:T(128)}, f32[64,16,12]{2,1,0:T(8,128)S(1)}, ...), condition=%wide.region_2.3_spmd, body=%wide.region_1.2_spmd.sunk | while | flops 393221 | bytes 2558343 | solution.py:38
  216.7 1.5 bitcast_add_fusion.3
  218.4 1.5 bitcast_add_fusion.3
  220.1 1.5 bitcast_add_fusion.3
  221.8 1.5 bitcast_add_fusion.3
  223.6 1.5 bitcast_add_fusion.3
  225.3 1.5 bitcast_add_fusion.3
  227.0 1.5 bitcast_add_fusion.3
  228.8 1.5 bitcast_add_fusion.3
  230.5 1.5 bitcast_add_fusion.3
  232.2 1.5 bitcast_add_fusion.3
  233.9 1.5 bitcast_add_fusion.3
  235.7 1.5 bitcast_add_fusion.3
  237.4 1.5 bitcast_add_fusion.3
  239.1 1.5 bitcast_add_fusion.3
  240.9 1.5 bitcast_add_fusion.3
  242.6 1.5 bitcast_add_fusion.3
  244.3 1.5 bitcast_add_fusion.3
  246.0 1.5 bitcast_add_fusion.3
  247.8 1.5 bitcast_add_fusion.3
  249.5 1.5 bitcast_add_fusion.3
  251.2 1.5 bitcast_add_fusion.3
  252.9 1.5 bitcast_add_fusion.3
  254.7 1.5 bitcast_add_fusion.3
  256.4 1.5 bitcast_add_fusion.3
  258.1 1.5 bitcast_add_fusion.3
  259.9 1.5 bitcast_add_fusion.3
  261.6 1.5 bitcast_add_fusion.3
  263.3 1.5 bitcast_add_fusion.3
  265.0 1.5 bitcast_add_fusion.3
  266.8 1.5 bitcast_add_fusion.3
  278.9 1.5 bitcast_add_fusion.3
  311.7 1.5 bitcast_add_fusion.3
  326.1 45.1 %while.25 = (s32[]{:T(128)}, f32[16,16,12,64]{3,2,1,0:T(8,128)S(1)}, f32[8,16,12,64]{3,2,1,0:T(8,128)}, f32[8,16,12]{2,1,0:T(8,128)}, f32[8,16,12]{2,1,0:T(8,128...) while((s32[]{:T(128)}, ...), condition=%wide.region_4.5_spmd, body=%wide.region_3.4_spmd.sunk | while | flops 2985986 | bytes 4193969 | solution.py:121
  330.1 1.6 bitcast_dynamic-update-slice_fusion.2
  335.8 1.6 bitcast_dynamic-update-slice_fusion.2
  341.4 1.6 bitcast_dynamic-update-slice_fusion.2
  347.1 1.6 bitcast_dynamic-update-slice_fusion.2
  352.7 1.6 bitcast_dynamic-update-slice_fusion.2
  358.3 1.6 bitcast_dynamic-update-slice_fusion.2
  364.0 1.6 bitcast_dynamic-update-slice_fusion.2
  369.6 1.6 bitcast_dynamic-update-slice_fusion.2
  371.2 1.6 reshape.99
  (318 shorter events, 102.9 us)
Async XLA Ops:
  6.5 1.3 copy-start
  6.5 8.4 %copy-start.5 = (bf16[8,1,16,768]{3,2,1,0:T(8,128)(2,1)S(1)}, bf16[8,1,16,768]{3,2,1,0:T(8,128)(2,1)}, u32[]{:S(2)}) copy-start(bf16[8,1,16,768]{3,2,1,0:T(8,128)(2,1)} %param.14) | copy-start | bytes 589828
  6.5 8.3 %copy-start.7 = (f32[3,3,800]{2,1,0:T(4,128)S(1)}, f32[3,3,800]{2,1,0:T(4,128)}, u32[]{:S(2)}) copy-start(f32[3,3,800]{2,1,0:T(4,128)} %param.17) | copy-start | bytes 86404
  6.5 8.4 %copy-start.4 = (bf16[768,780]{0,1:T(8,128)(2,1)S(1)}, bf16[768,780]{0,1:T(8,128)(2,1)}, u32[]{:S(2)}) copy-start(bf16[768,780]{0,1:T(8,128)(2,1)} %param.16) | copy-start | bytes 3594244
  6.5 209.8 %all-gather.2.cloned.1.call-start = ((), (), s32[]{:S(2)}) async-start(), calls=%async_computation | async-start | bytes 51118080 | tf_op jit(solution)/shard_map/all_gather | solution.py:30
  9.3 6.2 %copy-start.11 = (f32[12]{0:T(128)S(1)}, f32[12]{0:T(128)}, u32[]{:S(2)}) copy-start(f32[12]{0:T(128)} %param.19) | copy-start | bytes 148
  9.3 6.4 %copy-start.10 = (f32[12]{0:T(128)S(1)}, f32[12]{0:T(128)}, u32[]{:S(2)}) copy-start(f32[12]{0:T(128)} %param.20) | copy-start | bytes 148
  9.5 8.4 %collective-permute-start.1 = (bf16[8,1,16,800]{3,0,2,1:T(8,128)(2,1)S(1)}, bf16[8,1,16,800]{3,0,2,1:T(8,128)(2,1)S(1)}, u32[]{:S(2)}, u32[]{:S(2)}) collective-permute-start(bf16[8,1,16,800]{3,0,2,1:T(8,128)(2,1)S(1)} %copy.40), channel_id=1, source_target_pairs={{1,0},{2,1},{3,2},{4,3},{5,4},{6,5},{7,6},{9,8},{10,9},{11,10},{12... | collective-permute-start | bytes 614408 | tf_op jit(solution)/shard_map/ppermute | solution.py:23
  10.8 7.9 %collective-permute-start = (bf16[8,1,16,800]{3,0,2,1:T(8,128)(2,1)S(1)}, bf16[8,1,16,800]{3,0,2,1:T(8,128)(2,1)S(1)}, u32[]{:S(2)}, u32[]{:S(2)}) collective-permute-start(bf16[8,1,16,800]{3,0,2,1:T(8,128)(2,1)S(1)} %copy.40), channel_id=1, source_target_pairs={{0,1},{1,2},{2,3},{3,4},{4,5},{5,6},{6,7},{8,9},{9,10},{10,11},{11... | collective-permute-start | bytes 614408 | tf_op jit(solution)/shard_map/ppermute | solution.py:20
  15.4 3.4 copy-start.9
  19.2 0.8 copy-start.3
  19.7 2.1 copy-start.2
  325.5 0.7 copy-start.8
  371.2 2.0 copy-start.6
  371.2 2.0 copy-start.12
  371.2 2.0 copy-start.13
  373.2 1.3 copy-start.1
Sparse Core Ops, SparseCore 0:
  23.8 192.4 all-gather.1
where the time goes:
time: 385 us; the launch traced here: 381 us
  waiting for transfers between devices  144 us (37%)
  other arithmetic  125 us (32%)
  blocking collectives  49.5 us (13%)
  local copies, waits for them, and re-layouts  25 us (6%)
  matrix products  15.1 us (4%)
  between operations  13.7 us (4%)
  starting transfers between devices  5.32 us (1%)
    all_gather x1, waiting for transfers between devices, carried_in(): gathered = jax.tree.map(lambda a: lax.all_gather(a, axis), part)  142 us
    add x63, other arithmetic, combine_blocks(): carried.reshape(following[1].shape) + following[1]  94.4 us
    all_gather x1, blocking collectives, carried_in(): gathered = jax.tree.map(lambda a: lax.all_gather(a, axis), part)  49.5 us
    dynamic_update_slice x8, other arithmetic, per_device(): lax.scan(advance, incoming, (jnp.exp(log_decay), step_size, values, write...  13.1 us
    mul x189, local copies, waits for them, and re-layouts, combine_blocks(): earlier[1].reshape(earlier[1].shape[0], NSTATE, HEADS, HEAD_DIM)  11.7 us
    dot_general x8, matrix products, advance(): jnp.einsum('cn,cnhp->chp', read_now, carry_state, precision=lax.Precision...  10.4 us
    mul x8, other arithmetic, advance(): step_now[:, :, None] * value_now  7.97 us
  transfers between devices with their start and end apart: 3, of which 3 were waited for; matrix products, arithmetic and copies ran while one was open for 1% of the time, Pallas kernels for 0%

commit v1 on v0

v1 whole, which is shorter than its diff:
```python
import functools

import jax
import jax.numpy as jnp
from jax import lax
from jax.experimental import pallas as pl
from jax.experimental.pallas import tpu as pltpu
from jax.sharding import PartitionSpec as P

D = 768
HEADS = 12
GW = 16
INNER = 768
CONV_CH = 800
F = 8
T = F * GW
BLOCKS = 64
CHUNK = 128
EXTRA = 64
STEP = 96

f32 = jnp.float32
bf16 = jnp.bfloat16


def lanes(rows):
    return lax.broadcasted_iota(jnp.int32, (rows, 128), 1)


def dot(a, b, dims=((1,), (0,)), precision=None):
    return lax.dot_general(a, b, (dims, ((), ())), preferred_element_type=f32, precision=precision)


def cell_major():
    r = lax.broadcasted_iota(jnp.int32, (T, T), 0)
    s = lax.broadcasted_iota(jnp.int32, (T, T), 1)
    return jnp.where(s == (r & (F - 1)) * GW + (r >> 3), 1.0, 0.0).astype(bf16)


def frame_major():
    r = lax.broadcasted_iota(jnp.int32, (T, T), 0)
    s = lax.broadcasted_iota(jnp.int32, (T, T), 1)
    return jnp.where(s == (r & (GW - 1)) * F + (r >> 4), 1.0, 0.0).astype(bf16)


def silu(x):
    return x / (1.0 + jnp.exp(-x))


def softplus(x):
    return jnp.maximum(x, 0.0) + jnp.log1p(jnp.exp(-jnp.abs(x)))


def convolve(rows, taps, bias):
    part = []
    for j in range(3):
        part.append(taps[0][j] * rows[0] + taps[1][j] * rows[1] + taps[2][j] * rows[2])
    edge = jnp.zeros((F, rows[0].shape[1]), f32)
    left = jnp.concatenate([edge, part[0][: T - F]], axis=0)
    right = jnp.concatenate([part[2][F:], edge], axis=0)
    return silu(part[1] + left + right + bias)


def second_half(q, tile, keys, steps):
    lane = lanes(T)
    if q % 2:
        tile = pltpu.roll(tile, 64, 1)
    return jnp.where(
        lane < EXTRA,
        tile,
        jnp.where(
            lane < STEP,
            keys,
            jnp.where(
                lane < STEP + 2,
                pltpu.roll(steps, STEP - 2 * q, 1),
                pltpu.roll(steps, STEP + 2 - (8 + q), 1),
            ),
        ),
    )


def packets(first, second):
    n = first.shape[0] // F
    return jnp.concatenate(
        [first.reshape(n, F, 128), second.reshape(n, F, 128)], axis=1
    ).astype(bf16)


def scan_frames(chunks, bias_lane, rate_lane):
    lane = lanes(CHUNK)
    r = lax.broadcasted_iota(jnp.int32, (CHUNK, CHUNK), 0)
    s = lax.broadcasted_iota(jnp.int32, (CHUNK, CHUNK), 1)
    past = s <= r
    tri = jnp.where(past, 1.0, 0.0).astype(f32)
    half = lane < 64
    state1 = jnp.zeros((128, 128), f32)
    state2 = jnp.zeros((128, 128), f32)
    outs = []
    for x1, x2 in chunks:
        step = softplus(x2 + bias_lane)
        cum = dot(tri, -step * rate_lane, precision=lax.Precision.HIGHEST)
        late = jnp.transpose(jnp.log(step) - cum)
        write = jnp.where((lane >= EXTRA) & (lane < EXTRA + 16), x2, 0.0).astype(bf16)
        read = pltpu.roll(x2, 112, 1).astype(bf16)
        pair = dot(read, write, ((1,), (1,)))
        end = cum[CHUNK - 1 :, :]
        weight = jnp.exp(end - cum) * step
        reach = jnp.exp(cum)
        x1b, x2b = x1.astype(bf16), x2.astype(bf16)
        inner = []
        for k, x in enumerate((x1b, x1b, x2b)):
            span = cum[:, STEP + k : STEP + k + 1] + late[STEP + k : STEP + k + 1, :]
            m = pair * jnp.exp(jnp.where(past, span, -1e30))
            inner.append(dot(m.astype(bf16), x))

        def col(a, k):
            return a[:, STEP + k : STEP + k + 1]

        y1 = jnp.where(half, inner[0], inner[1])
        y1 = y1 + jnp.where(half, col(reach, 0), col(reach, 1)) * dot(read, state1.astype(bf16))
        y2 = inner[2] + col(reach, 2) * dot(read, state2.astype(bf16))
        w1 = (x1 * jnp.where(half, col(weight, 0), col(weight, 1))).astype(bf16)
        w2 = (x2 * col(weight, 2)).astype(bf16)
        fade = jnp.exp(end)
        half1 = half[:1]
        state1 = state1 * jnp.where(half1, col(fade, 0), col(fade, 1)) + dot(write, w1, ((0,), (0,)))
        state2 = state2 * col(fade, 2) + dot(write, w2, ((0,), (0,)))
        outs.append((y1, y2))
    return outs


def kernel(
    n_tm,
    n_row,
    tok_hbm,
    mix_hbm,
    gate_hbm,
    out_hbm,
    taps_ref,
    cbias_ref,
    gain_ref,
    sbias_ref,
    rate_ref,
    skip_ref,
    o_ref,
    tok,
    halo,
    mixw,
    gatew,
    outw,
    value,
    gate,
    send1,
    recv1,
    send2,
    recv2,
    load_sem,
    halo_send,
    halo_recv,
    a2a_send,
    a2a_recv,
):
    me = lax.axis_index("tm")
    row = lax.axis_index("row")
    up = lax.rem(row + 1, n_row)
    down = lax.rem(row + n_row - 1, n_row)

    loads = [
        pltpu.make_async_copy(src, dst, load_sem.at[i])
        for i, (src, dst) in enumerate(
            ((tok_hbm, tok), (mix_hbm, mixw), (gate_hbm, gatew), (out_hbm, outw))
        )
    ]
    for load in loads:
        load.start()

    barrier = pltpu.get_barrier_semaphore()
    for other in (up, down):
        pl.semaphore_signal(barrier, inc=1, device_id={"row": other})

    def greet(i, c):
        pl.semaphore_signal(barrier, inc=1, device_id={"tm": lax.rem(me + i, n_tm)})
        return c

    lax.fori_loop(1, n_tm, greet, 0)
    pl.semaphore_wait(barrier, n_tm + 1)

    halos = [
        pltpu.make_async_remote_copy(
            src_ref=tok_hbm,
            dst_ref=halo.at[i],
            send_sem=halo_send.at[i],
            recv_sem=halo_recv.at[i],
            device_id={"row": other},
        )
        for i, other in enumerate((up, down))
    ]
    for copy in halos:
        copy.start()

    perm = cell_major()
    loads[0].wait()
    own = dot(perm, tok[...]).astype(bf16)
    loads[1].wait()
    loads[2].wait()
    gs = dot(own, gatew[...]).astype(bf16).astype(f32)
    gate[...] = gs[:, :INNER]
    steps = jnp.concatenate([gs[:, INNER:], jnp.zeros((T, 128 - HEADS), f32)], axis=1)
    for copy in halos:
        copy.wait()
    low = jnp.where(row > 0, dot(perm, halo[0]), 0.0).astype(bf16)
    high = jnp.where(row < n_row - 1, dot(perm, halo[1]), 0.0).astype(bf16)
    stacked = jnp.concatenate([low, own, high], axis=0)

    def activated(start, size):
        z = dot(stacked, mixw[:, start : start + size]).astype(bf16).astype(f32)
        taps = [[taps_ref[i, j : j + 1, start : start + size] for j in range(3)] for i in range(3)]
        return convolve([z[:T], z[T : 2 * T], z[2 * T :]], taps, cbias_ref[:, start : start + size])

    key = activated(INNER, 32)
    key = jnp.concatenate([key, jnp.zeros((T, 96), f32)], axis=1)
    key = pltpu.roll(key, EXTRA, 1)
    for g in range(3):
        value[:, 256 * g : 256 * (g + 1)] = activated(256 * g, 256)
    for q in range(4):
        tile = value[:, 128 * (4 + q // 2) : 128 * (5 + q // 2)]
        send1[GW * q : GW * (q + 1)] = packets(
            value[:, 128 * q : 128 * (q + 1)], second_half(q, tile, key, steps)
        )

    def exchange(send, recv, which):
        def one(i, c):
            other = lax.rem(me + i, n_tm)
            pltpu.make_async_remote_copy(
                src_ref=send.at[other],
                dst_ref=recv.at[me],
                send_sem=a2a_send.at[which],
                recv_sem=a2a_recv.at[which],
                device_id={"tm": other},
            ).start()
            return c

        lax.fori_loop(1, n_tm, one, 0)
        recv[me] = send[me]
        every = recv.at[pl.ds(0, n_tm - 1)]
        pltpu.make_async_copy(every, every, a2a_recv.at[which]).wait()

    exchange(send1, recv1, 0)

    q = me // GW
    lane = lanes(1)
    bias_lane = jnp.zeros((1, 128), f32)
    rate_lane = jnp.zeros((1, 128), f32)
    for k, head in enumerate((2 * q, 2 * q + 1, 8 + q)):
        bias_lane = jnp.where(lane == STEP + k, sbias_ref[head], bias_lane)
        rate_lane = jnp.where(lane == STEP + k, rate_ref[head], rate_lane)
    chunks = []
    per = CHUNK // F
    for c in range(n_tm // per):
        block = recv1[per * c : per * (c + 1)].astype(f32)
        chunks.append((block[:, :F].reshape(CHUNK, 128), block[:, F:].reshape(CHUNK, 128)))
    for c, (y1, y2) in enumerate(scan_frames(chunks, bias_lane, rate_lane)):
        send2[per * c : per * (c + 1)] = packets(y1, y2)

    exchange(send2, recv2, 1)

    firsts, thirds = [], []
    for q in range(4):
        block = recv2[GW * q : GW * (q + 1)].astype(f32)
        firsts.append(block[:, :F].reshape(T, 128))
        thirds.append(block[:, F:].reshape(T, 128))
    lane = lanes(T)
    for q in (0, 2):
        firsts.append(jnp.where(lane < 64, thirds[q], pltpu.roll(thirds[q + 1], 64, 1)))
    gated = []
    total = jnp.zeros((T, 1), f32)
    for j in range(6):
        cut = slice(128 * j, 128 * (j + 1))
        skip = jnp.where(lane < 64, skip_ref[2 * j], skip_ref[2 * j + 1])
        g = (firsts[j] + skip * value[:, cut]) * silu(gate[:, cut])
        total = total + jnp.sum(g * g, axis=-1, keepdims=True)
        gated.append(g)
    scale = lax.rsqrt(total * (1.0 / INNER) + 1e-5)
    normed = jnp.concatenate(
        [gated[j] * scale * gain_ref[:, 128 * j : 128 * (j + 1)] for j in range(6)], axis=1
    ).astype(bf16)
    normed = dot(frame_major(), normed).astype(bf16)
    loads[3].wait()
    o_ref[...] = (tok[...].astype(f32) + dot(normed, outw[...])).astype(bf16)

    for which, send in ((0, send1), (1, send2)):
        every = send.at[pl.ds(0, n_tm - 1)]
        pltpu.make_async_copy(every, every, a2a_send.at[which]).wait()


def per_device(
    n_tm,
    n_row,
    depth_tokens,
    mixer_weight,
    gate_weight,
    conv_kernel,
    conv_bias,
    step_bias,
    decay_rate,
    skip_gain,
    norm_gain,
    out_weight,
):
    hbm = pl.BlockSpec(memory_space=pl.ANY)
    vmem = pl.BlockSpec(memory_space=pltpu.VMEM)
    smem = pl.BlockSpec(memory_space=pltpu.SMEM)
    out = pl.pallas_call(
        functools.partial(kernel, n_tm, n_row),
        out_shape=jax.ShapeDtypeStruct((T, D), bf16),
        in_specs=[hbm] * 4 + [vmem] * 3 + [smem] * 3,
        out_specs=vmem,
        scratch_shapes=[
            pltpu.VMEM((T, D), bf16),
            pltpu.VMEM((2, T, D), bf16),
            pltpu.VMEM((D, CONV_CH), bf16),
            pltpu.VMEM((D, INNER + HEADS), bf16),
            pltpu.VMEM((INNER, D), bf16),
            pltpu.VMEM((T, INNER), f32),
            pltpu.VMEM((T, INNER), f32),
            pltpu.VMEM((BLOCKS, 2 * F, 128), bf16),
            pltpu.VMEM((BLOCKS, 2 * F, 128), bf16),
            pltpu.VMEM((BLOCKS, 2 * F, 128), bf16),
            pltpu.VMEM((BLOCKS, 2 * F, 128), bf16),
            pltpu.SemaphoreType.DMA((4,)),
            pltpu.SemaphoreType.DMA((2,)),
            pltpu.SemaphoreType.DMA((2,)),
            pltpu.SemaphoreType.DMA((2,)),
            pltpu.SemaphoreType.DMA((2,)),
        ],
        compiler_params=pltpu.CompilerParams(
            collective_id=0, has_side_effects=True, vmem_limit_bytes=48 * 1024 * 1024
        ),
    )(
        depth_tokens.reshape(T, D),
        mixer_weight,
        gate_weight,
        out_weight,
        conv_kernel,
        conv_bias.reshape(1, CONV_CH),
        norm_gain.reshape(1, INNER),
        step_bias,
        decay_rate,
        skip_gain,
    )
    return out.reshape(depth_tokens.shape)


def solution(mesh):
    placed = (P("tm", "row", None, None), P(), P(), P(), P(), P(), P(), P(), P(), P())
    return jax.shard_map(
        functools.partial(per_device, mesh.shape["tm"], mesh.shape["row"]),
        mesh=mesh,
        in_specs=placed,
        out_specs=P("tm", "row", None, None),
        check_vma=False,
    )
```

time: 385 us -> 53.6 us (0.14)
  the two profiles are of different devices: /device:TPU:455 before, /device:TPU:1 now
where the time goes in v1:
time: 53.6 us; the launch traced here: 53.3 us
  Pallas kernels  46.2 us (86%)
  local copies, waits for them, and re-layouts  7 us (13%)
    pallas_call x1, Pallas kernels, per_device(): pl.pallas_call(functools.partial(kernel, n_tm, n_row), out_shape=jax.Shap...  46.2 us
    unnamed x15, local copies, waits for them, and re-layouts  5.62 us

profile of v1, /device:TPU:1, one launch (start us, length us, event | category | flops | bytes accessed | tf_op | source)
XLA Modules:
  0.0 53.3 jit_solution(7676144673403787853)
XLA Ops:
  0.0 0.7 %reshape.14.gain_ref = f32[1,768]{1,0:T(1,128)S(1)} reshape(f32[768]{0:T(1024)} %param.18) | data formatting | bytes 6144 | tf_op jit(solution)/shard_map/reshape | solution.py:347
  0.7 0.7 %reshape.13.cbias_ref = f32[1,800]{1,0:T(1,128)S(1)} reshape(f32[800]{0:T(1024)} %param.14) | data formatting | bytes 6400 | tf_op jit(solution)/shard_map/reshape | solution.py:346
  1.4 1.8 %copy.11.mix_hbm = bf16[768,800]{1,0:T(8,128)(2,1)S(1)} copy(bf16[768,800]{0,1:T(8,128)(2,1)} %param.11) | data formatting | bytes 2457600 | tf_op args[1]
  3.1 0.0 copy-start.1
  3.2 0.0 copy-start.2
  3.2 0.0 copy-start.3
  3.2 0.0 copy-start.4
  3.2 0.0 copy-start.5
  3.2 1.9 %copy.12.gate_hbm = bf16[768,780]{1,0:T(8,128)(2,1)S(1)} copy(bf16[768,780]{0,1:T(8,128)(2,1)} %param.12) | data formatting | bytes 2396160 | tf_op args[2]
  5.1 0.0 copy-done.1
  5.1 0.0 copy-done.2
  5.1 0.0 copy-done.3
  5.1 0.0 copy-done.4
  5.1 0.0 copy-done.5
  5.2 0.0 copy-start
  5.2 1.3 %copy-done = bf16[768,768]{1,0:T(8,128)(2,1)S(1)} copy-done((bf16[768,768]{1,0:T(8,128)(2,1)S(1)}, bf16[768,768]{1,0:T(8,128)(2,1)}, u32[]{:S(2)}) %copy-start) | copy-done | bytes 1179672
  6.4 46.2 %shard_map.100 = bf16[128,768]{1,0:T(8,128)(2,1)S(1)} custom-call(bf16[128,768]{1,0:T(8,128)(2,1)S(1)} %bitcast.5, bf16[768,800]{1,0:T(8,128)(2,1)S(1)} %copy.11.mix_hbm, bf16[768,780]{1,0:T(8,128)(2,1)S(1)} %copy.12.gate_hbm, bf16[768,768]{1,0:T(8,128)(2,1)S(1)} %copy-done, f32[3,3,800]{2,1,0:T(4,128)S(1)} %copy-done.2, f32[1,800]{1,0:T(1,128)S(1)} %reshape.13.cbias_ref, ...), custom_call_target="tpu_custom_call" | custom-call | tf_op jit(solution)/shard_map/pallas_call | solution.py:314
  52.7 0.7 %copy.15 = bf16[8,1,16,768]{3,2,1,0:T(8,128)(2,1)} copy(bf16[8,1,16,768]{3,2,1,0:T(8,128)(2,1)S(1)} %bitcast.4) | data formatting | bytes 393216
Async XLA Ops:
  3.1 2.0 %copy-start.1 = (bf16[8,1,16,768]{3,2,1,0:T(8,128)(2,1)S(1)}, bf16[8,1,16,768]{3,2,1,0:T(8,128)(2,1)}, u32[]{:S(2)}) copy-start(bf16[8,1,16,768]{3,2,1,0:T(8,128)(2,1)} %param.10) | copy-start | bytes 589828
  3.2 2.0 %copy-start.2 = (f32[3,3,800]{2,1,0:T(4,128)S(1)}, f32[3,3,800]{2,1,0:T(4,128)}, u32[]{:S(2)}) copy-start(f32[3,3,800]{2,1,0:T(4,128)} %taps_ref.1) | copy-start | bytes 86404
  3.2 1.9 %copy-start.3 = (f32[12]{0:T(128)S(1)}, f32[12]{0:T(128)}, u32[]{:S(2)}) copy-start(f32[12]{0:T(128)} %sbias_ref.1) | copy-start | bytes 148
  3.2 1.9 %copy-start.4 = (f32[12]{0:T(128)S(1)}, f32[12]{0:T(128)}, u32[]{:S(2)}) copy-start(f32[12]{0:T(128)} %rate_ref.1) | copy-start | bytes 148
  3.2 1.9 %copy-start.5 = (f32[12]{0:T(128)S(1)}, f32[12]{0:T(128)}, u32[]{:S(2)}) copy-start(f32[12]{0:T(128)} %skip_ref.1) | copy-start | bytes 148
  5.2 1.3 %copy-start = (bf16[768,768]{1,0:T(8,128)(2,1)S(1)}, bf16[768,768]{1,0:T(8,128)(2,1)}, u32[]{:S(2)}) copy-start(bf16[768,768]{1,0:T(8,128)(2,1)} %out_hbm.1) | copy-start | bytes 3538948

commit v2 on v1

v2 whole, which is shorter than its diff:
```python
import functools

import jax
import jax.numpy as jnp
from jax import lax
from jax.experimental import pallas as pl
from jax.experimental.pallas import tpu as pltpu
from jax.sharding import PartitionSpec as P

D = 768
HEADS = 12
NSTATE = 16
GW = 16
INNER = 768
CONV_CH = 800
F = 8
T = F * GW
GROUP = 16
SPAN = 128
KEY = 0
STEP = 32

NT = ((1,), (1,))
TN = ((0,), (0,))
f32 = jnp.float32
bf16 = jnp.bfloat16


def lanes(rows):
    return lax.broadcasted_iota(jnp.int32, (rows, 128), 1)


def dot(a, b, dims=((1,), (0,)), precision=None):
    return lax.dot_general(a, b, (dims, ((), ())), preferred_element_type=f32, precision=precision)


def cell_major():
    r = lax.broadcasted_iota(jnp.int32, (T, T), 0)
    s = lax.broadcasted_iota(jnp.int32, (T, T), 1)
    return jnp.where(s == (r & (F - 1)) * GW + (r >> 3), 1.0, 0.0).astype(bf16)


def frame_major():
    r = lax.broadcasted_iota(jnp.int32, (T, T), 0)
    s = lax.broadcasted_iota(jnp.int32, (T, T), 1)
    return jnp.where(s == (r & (GW - 1)) * F + (r >> 4), 1.0, 0.0).astype(bf16)


def silu(x):
    return x / (1.0 + jnp.exp(-x))


def softplus(x):
    return jnp.maximum(x, 0.0) + jnp.log1p(jnp.exp(-jnp.abs(x)))


def convolve(rows, taps, bias):
    part = []
    for j in range(3):
        part.append(taps[0][j] * rows[0] + taps[1][j] * rows[1] + taps[2][j] * rows[2])
    edge = jnp.zeros((F, rows[0].shape[1]), f32)
    left = jnp.concatenate([edge, part[0][: T - F]], axis=0)
    right = jnp.concatenate([part[2][F:], edge], axis=0)
    return silu(part[1] + left + right + bias)


def packets(tiles):
    return jnp.concatenate([t.reshape(GW, F, 128) for t in tiles], axis=1).astype(bf16)


def unpack(block, j):
    return block[:, F * j : F * (j + 1)].reshape(SPAN, 128)


def kernel(
    n_tm,
    n_row,
    tok_hbm,
    mix_hbm,
    gate_hbm,
    out_hbm,
    taps_hbm,
    cbias_hbm,
    gain_hbm,
    sbias_ref,
    rate_ref,
    skip_ref,
    o_ref,
    tok,
    halo,
    mixw,
    gatew,
    outw,
    taps_ref,
    cbias_ref,
    gain_ref,
    center,
    value,
    gate,
    send1,
    recv1,
    state_out,
    state_in,
    fade_out,
    fade_in,
    send2,
    recv2,
    load_sem,
    halo_send,
    halo_recv,
    one_send,
    one_recv,
    state_send,
    state_recv,
    two_send,
    two_recv,
):
    me = lax.axis_index("tm")
    row = lax.axis_index("row")
    up = lax.rem(row + 1, n_row)
    down = lax.rem(row + n_row - 1, n_row)
    n_groups = n_tm // GROUP
    group = me // GROUP
    member = lax.rem(me, GROUP)

    def peer(i):
        return lax.rem(member + i, GROUP)

    barrier = pltpu.get_barrier_semaphore()
    for other in (up, down):
        pl.semaphore_signal(barrier, inc=1, device_id={"row": other})

    def greet(i, c):
        pl.semaphore_signal(barrier, inc=1, device_id={"tm": group * GROUP + peer(i)})
        return c

    lax.fori_loop(1, GROUP, greet, 0)
    for i in range(1, n_groups):
        pl.semaphore_signal(barrier, inc=1, device_id={"tm": lax.rem(me + GROUP * i, n_tm)})

    loads = [
        pltpu.make_async_copy(src, dst, load_sem.at[i])
        for i, (src, dst) in enumerate(
            (
                (tok_hbm, tok),
                (gate_hbm, gatew),
                (mix_hbm, mixw),
                (taps_hbm, taps_ref),
                (cbias_hbm, cbias_ref),
                (gain_hbm, gain_ref),
                (out_hbm, outw),
            )
        )
    ]
    for load in loads:
        load.start()
    pl.semaphore_wait(barrier, 2 + GROUP - 1 + n_groups - 1)

    halos = [
        pltpu.make_async_remote_copy(
            src_ref=tok_hbm,
            dst_ref=halo.at[i],
            send_sem=halo_send.at[i],
            recv_sem=halo_recv.at[i],
            device_id={"row": other},
        )
        for i, other in enumerate((up, down))
    ]
    for copy in halos:
        copy.start()

    perm = cell_major()
    loads[0].wait()
    own = dot(perm, tok[...]).astype(bf16)
    loads[1].wait()
    gs = dot(own, gatew[...], NT).astype(bf16).astype(f32)
    gate[...] = gs[:, :INNER]
    steps = jnp.concatenate([gs[:, INNER:], jnp.zeros((T, 128 - HEADS), f32)], axis=1)
    steps = pltpu.roll(steps, STEP, 1)
    loads[2].wait()
    center[...] = dot(own, mixw[...], NT).astype(bf16).astype(f32)
    for load in loads[3:5]:
        load.wait()

    for copy in halos:
        copy.wait()
    low = jnp.where(row > 0, dot(perm, halo[0]), 0.0).astype(bf16)
    high = jnp.where(row < n_row - 1, dot(perm, halo[1]), 0.0).astype(bf16)
    sides = jnp.concatenate([low, high], axis=0)

    def activated(start, size):
        z = dot(sides, mixw[start : start + size, :], NT).astype(bf16).astype(f32)
        taps = [[taps_ref[i, j : j + 1, start : start + size] for j in range(3)] for i in range(3)]
        rows = [z[:T], center[:, start : start + size], z[T:]]
        return convolve(rows, taps, cbias_ref[start : start + size].reshape(1, size))

    def send_all(send, recv, send_sem, recv_sem):
        def one(i, c):
            other = peer(i)
            pltpu.make_async_remote_copy(
                src_ref=send.at[other],
                dst_ref=recv.at[member],
                send_sem=send_sem,
                recv_sem=recv_sem,
                device_id={"tm": group * GROUP + other},
            ).start()
            return c

        lax.fori_loop(1, GROUP, one, 0)
        recv[member] = send[member]

    def wait_all(buf, sem, count=GROUP - 1):
        every = buf.at[pl.ds(0, count)]
        pltpu.make_async_copy(every, every, sem).wait()

    key = activated(INNER, 32)
    key = jnp.concatenate([key, jnp.zeros((T, 96), f32)], axis=1)
    extra = jnp.where(lanes(T) < STEP, key, steps)
    first = activated(0, 384)
    value[:, :384] = first
    send1[0] = packets([extra] + [first[:, 128 * j : 128 * (j + 1)] for j in range(3)])
    send_all(send1.at[0], recv1.at[0], one_send.at[0], one_recv.at[0])
    second = activated(384, 384)
    value[:, 384:] = second
    send1[1] = packets(
        [second[:, 128 * j : 128 * (j + 1)] for j in range(3)] + [jnp.zeros((T, 128), f32)]
    )
    send_all(send1.at[1], recv1.at[1], one_send.at[1], one_recv.at[1])

    lane = lanes(1)
    bias_lane = jnp.zeros((1, 128), f32)
    rate_lane = jnp.zeros((1, 128), f32)
    for h in range(HEADS):
        bias_lane = jnp.where(lane == STEP + h, sbias_ref[h], bias_lane)
        rate_lane = jnp.where(lane == STEP + h, rate_ref[h], rate_lane)
    r = lax.broadcasted_iota(jnp.int32, (SPAN, SPAN), 0)
    s = lax.broadcasted_iota(jnp.int32, (SPAN, SPAN), 1)
    past = s <= r
    half = lanes(SPAN) < 64

    def col(a, h):
        return a[:, STEP + h : STEP + h + 1]

    def both(a, j):
        return jnp.where(half[: a.shape[0]], col(a, 2 * j), col(a, 2 * j + 1))

    def send_state(part):
        for i in range(1, n_groups):
            pltpu.make_async_remote_copy(
                src_ref=state_out.at[part],
                dst_ref=state_in.at[part, i - 1],
                send_sem=state_send.at[part],
                recv_sem=state_recv.at[part],
                device_id={"tm": lax.rem(me + GROUP * i, n_tm)},
            ).start()

    wait_all(recv1.at[0], one_recv.at[0])
    block = recv1[0].astype(f32)
    extra = unpack(block, 0)
    x = [unpack(block, j) for j in range(1, 4)]
    step = softplus(extra + bias_lane)
    tri = jnp.where(past, 1.0, 0.0).astype(f32)
    cum = dot(tri, -step * rate_lane, precision=lax.Precision.HIGHEST)
    end = cum[SPAN - 1 :, :]
    fade_out[...] = jnp.broadcast_to(end, (8, 128))
    for i in range(1, n_groups):
        pltpu.make_async_remote_copy(
            src_ref=fade_out,
            dst_ref=fade_in.at[i - 1],
            send_sem=state_send.at[2],
            recv_sem=state_recv.at[2],
            device_id={"tm": lax.rem(me + GROUP * i, n_tm)},
        ).start()
    weight = jnp.exp(end - cum) * step
    write = extra[:, :NSTATE].astype(bf16)
    read = extra[:, NSTATE : 2 * NSTATE].astype(bf16)
    scaled = jnp.concatenate([x[j] * both(weight, j) for j in range(3)], axis=1).astype(bf16)
    state_out[0] = dot(write, scaled, TN).astype(bf16)
    send_state(0)
    wait_all(recv1.at[1], one_recv.at[1])
    block = recv1[1].astype(f32)
    x = x + [unpack(block, j) for j in range(3)]
    scaled = jnp.concatenate([x[j] * both(weight, j) for j in range(3, 6)], axis=1).astype(bf16)
    state_out[1] = dot(write, scaled, TN).astype(bf16)
    send_state(1)

    late = jnp.transpose(jnp.log(step) - cum)
    reach = jnp.exp(cum)
    pair = dot(read, write, NT)
    inner = []
    for j in range(6):
        xb = x[j].astype(bf16)
        part = []
        for h in (2 * j, 2 * j + 1):
            span = col(cum, h) + late[STEP + h : STEP + h + 1, :]
            m = pair * jnp.exp(jnp.where(past, span, -1e30))
            part.append(dot(m.astype(bf16), xb))
        inner.append(jnp.where(half, part[0], part[1]))

    wait_all(fade_in, state_recv.at[2], n_groups - 1)
    fades = [jnp.exp(fade_in[i][:1]) for i in range(n_groups - 1)]

    def arrived(part):
        wait_all(state_in.at[part], state_recv.at[part], n_groups - 1)
        total = jnp.zeros((NSTATE, 384), f32)
        for i in range(n_groups - 2, -1, -1):
            fade = jnp.concatenate([both(fades[i], 3 * part + j) for j in range(3)], axis=1)
            total = jnp.where(group > i, total * fade + state_in[part, i].astype(f32), 0.0)
        return dot(read, total.astype(bf16))

    def send_back(third, tiles):
        send2[third] = packets(tiles)
        send_all(send2.at[third], recv2.at[third], two_send.at[third], two_recv.at[third])

    def result(carried, j):
        k = j % 3
        return inner[j] + both(reach, j) * carried[:, 128 * k : 128 * (k + 1)]

    carried = arrived(0)
    send_back(0, [result(carried, 0), result(carried, 1)])
    third = result(carried, 2)
    carried = arrived(1)
    send_back(1, [third, result(carried, 3)])
    send_back(2, [result(carried, 4), result(carried, 5)])

    loads[5].wait()
    lane = lanes(1)
    gated = []
    total = jnp.zeros((T, 1), f32)
    for third in range(3):
        wait_all(recv2.at[third], two_recv.at[third])
        block = recv2[third].astype(f32)
        for k in range(2):
            j = 2 * third + k
            cut = slice(128 * j, 128 * (j + 1))
            skip = jnp.where(lane < 64, skip_ref[2 * j], skip_ref[2 * j + 1])
            g = (unpack(block, k) + skip * value[:, cut]) * silu(gate[:, cut])
            total = total + jnp.sum(g * g, axis=-1, keepdims=True)
            gated.append(g * gain_ref[cut].reshape(1, 128))
    scale = lax.rsqrt(total * (1.0 / INNER) + 1e-5)
    normed = jnp.concatenate([g * scale for g in gated], axis=1).astype(bf16)
    normed = dot(frame_major(), normed).astype(bf16)
    loads[6].wait()
    o_ref[...] = (tok[...].astype(f32) + dot(normed, outw[...])).astype(bf16)

    for part in range(2):
        wait_all(send1.at[part], one_send.at[part])
        wait_all(state_in.at[part], state_send.at[part], n_groups - 1)
    wait_all(fade_in, state_send.at[2], n_groups - 1)
    for third in range(3):
        wait_all(send2.at[third], two_send.at[third])


def per_device(
    n_tm,
    n_row,
    depth_tokens,
    mixer_weight,
    gate_weight,
    conv_kernel,
    conv_bias,
    step_bias,
    decay_rate,
    skip_gain,
    norm_gain,
    out_weight,
):
    hbm = pl.BlockSpec(memory_space=pl.ANY)
    vmem = pl.BlockSpec(memory_space=pltpu.VMEM)
    smem = pl.BlockSpec(memory_space=pltpu.SMEM)
    dma = pltpu.SemaphoreType.DMA
    n_groups = n_tm // GROUP
    out = pl.pallas_call(
        functools.partial(kernel, n_tm, n_row),
        out_shape=jax.ShapeDtypeStruct((T, D), bf16),
        in_specs=[hbm] * 7 + [smem] * 3,
        out_specs=vmem,
        scratch_shapes=[
            pltpu.VMEM((T, D), bf16),
            pltpu.VMEM((2, T, D), bf16),
            pltpu.VMEM((CONV_CH, D), bf16),
            pltpu.VMEM((INNER + HEADS, D), bf16),
            pltpu.VMEM((INNER, D), bf16),
            pltpu.VMEM((3, 3, CONV_CH), f32),
            pltpu.VMEM((CONV_CH,), f32),
            pltpu.VMEM((INNER,), f32),
            pltpu.VMEM((T, CONV_CH), f32),
            pltpu.VMEM((T, INNER), f32),
            pltpu.VMEM((T, INNER), f32),
            pltpu.VMEM((2, GROUP, 4 * F, 128), bf16),
            pltpu.VMEM((2, GROUP, 4 * F, 128), bf16),
            pltpu.VMEM((2, NSTATE, 384), bf16),
            pltpu.VMEM((2, n_groups - 1, NSTATE, 384), bf16),
            pltpu.VMEM((8, 128), f32),
            pltpu.VMEM((n_groups - 1, 8, 128), f32),
            pltpu.VMEM((3, GROUP, 2 * F, 128), bf16),
            pltpu.VMEM((3, GROUP, 2 * F, 128), bf16),
            dma((7,)),
            dma((2,)),
            dma((2,)),
            dma((2,)),
            dma((2,)),
            dma((3,)),
            dma((3,)),
            dma((3,)),
            dma((3,)),
        ],
        compiler_params=pltpu.CompilerParams(
            collective_id=0, has_side_effects=True, vmem_limit_bytes=60 * 1024 * 1024
        ),
    )(
        depth_tokens.reshape(T, D),
        mixer_weight.T,
        gate_weight.T,
        out_weight,
        conv_kernel,
        conv_bias,
        norm_gain,
        step_bias,
        decay_rate,
        skip_gain,
    )
    return out.reshape(depth_tokens.shape)


def solution(mesh):
    placed = (P("tm", "row", None, None), P(), P(), P(), P(), P(), P(), P(), P(), P())
    return jax.shard_map(
        functools.partial(per_device, mesh.shape["tm"], mesh.shape["row"]),
        mesh=mesh,
        in_specs=placed,
        out_specs=P("tm", "row", None, None),
        check_vma=False,
    )
```

time: 53.6 us -> 45.2 us (0.84)
  local copies, waits for them, and re-layouts: 7 us -> 1.62 us
  Pallas kernels: 46.2 us -> 43.5 us
    unnamed x15 -> x1, local copies, waits for them, and re-layouts: 5.62 us -> 1.62 us
    pallas_call x1, Pallas kernels: 46.2 us -> 43.5 us  [per_device(): pl.pallas_call(functools.partial(kernel, n_tm, n_row), out_shape=jax.Shap...]
    reshape x2 -> x0, local copies, waits for them, and re-layouts: 1.38 us -> none  [the longest x1 0.69 us: per_device(): conv_bias.reshape(1, CONV_CH)]
where the time goes in v2:
time: 45.2 us; the launch traced here: 45.1 us
  Pallas kernels  43.5 us (96%)
  local copies, waits for them, and re-layouts  1.62 us (4%)
    pallas_call x1, Pallas kernels, per_device(): pl.pallas_call(functools.partial(kernel, n_tm, n_row), out_shape=jax.Shap...  43.5 us
    unnamed x1, local copies, waits for them, and re-layouts  1.62 us

profile of v2, /device:TPU:1, one launch (start us, length us, event | category | flops | bytes accessed | tf_op | source)
XLA Modules:
  0.0 45.1 jit_solution(3147760390298124057)
XLA Ops:
  0.0 43.5 %shard_map.100 = bf16[128,768]{1,0:T(8,128)(2,1)} custom-call(bf16[128,768]{1,0:T(8,128)(2,1)} %bitcast.9, bf16[800,768]{1,0:T(8,128)(2,1)} %bitcast.6, bf16[780,768]{1,0:T(8,128)(2,1)} %bitcast.7, bf16[768,768]{1,0:T(8,128)(2,1)} %out_hbm.1, f32[3,3,800]{2,1,0:T(4,128)} %taps_hbm.1, f32[800]{0:T(1024)} %cbias_hbm.1, f32[768]{0:T(1024)} %gain_hbm.1, ...), custom_call_target="tpu_custom_call" | custom-call | tf_op jit(solution)/shard_map/pallas_call | solution.py:373
  43.5 1.6 %copy.13 = bf16[8,1,16,768]{3,2,1,0:T(8,128)(2,1)} copy(bf16[8,1,16,768]{3,2,1,0:T(8,128)(2,1)} %bitcast.8) | data formatting | bytes 393216

commit v3 on v2

--- a/solution.py
+++ b/solution.py
@@ -17,6 +17,8 @@
 T = F * GW
 GROUP = 16
 SPAN = 128
+HALF = 64
+PIECE = 80
 KEY = 0
 STEP = 32
 
@@ -54,18 +56,25 @@
     return jnp.maximum(x, 0.0) + jnp.log1p(jnp.exp(-jnp.abs(x)))
 
 
-def convolve(rows, taps, bias):
-    part = []
-    for j in range(3):
-        part.append(taps[0][j] * rows[0] + taps[1][j] * rows[1] + taps[2][j] * rows[2])
-    edge = jnp.zeros((F, rows[0].shape[1]), f32)
-    left = jnp.concatenate([edge, part[0][: T - F]], axis=0)
-    right = jnp.concatenate([part[2][F:], edge], axis=0)
-    return silu(part[1] + left + right + bias)
+def convolve(wave, rows, taps, bias):
+    low, high = HALF * wave, HALF * (wave + 1)
+
+    def part(j, start, stop):
+        z = [r(start, stop) for r in rows]
+        return taps[0][j] * z[0] + taps[1][j] * z[1] + taps[2][j] * z[2]
+
+    edge = jnp.zeros((F, bias.shape[1]), f32)
+    if wave == 0:
+        left = jnp.concatenate([edge, part(0, low, high - F)], axis=0)
+        right = part(2, low + F, high + F)
+    else:
+        left = part(0, low - F, high - F)
+        right = jnp.concatenate([part(2, low + F, high), edge], axis=0)
+    return silu(part(1, low, high) + left + right + bias)
 
 
 def packets(tiles):
-    return jnp.concatenate([t.reshape(GW, F, 128) for t in tiles], axis=1).astype(bf16)
+    return jnp.concatenate([t.reshape(-1, F, 128) for t in tiles], axis=1).astype(bf16)
 
 
 def unpack(block, j):
@@ -94,7 +103,9 @@
     taps_ref,
     cbias_ref,
     gain_ref,
+    mine,
     center,
+    side,
     value,
     gate,
     send1,
@@ -122,6 +133,9 @@
     n_groups = n_tm // GROUP
     group = me // GROUP
     member = lax.rem(me, GROUP)
+    chip = member // 2
+    core = lax.rem(member, 2)
+    cell = core * (GW // 2) + chip
 
     def peer(i):
         return lax.rem(member + i, GROUP)
@@ -154,24 +168,29 @@
     ]
     for load in loads:
         load.start()
-    pl.semaphore_wait(barrier, 2 + GROUP - 1 + n_groups - 1)
-
-    halos = [
-        pltpu.make_async_remote_copy(
-            src_ref=tok_hbm,
-            dst_ref=halo.at[i],
-            send_sem=halo_send.at[i],
-            recv_sem=halo_recv.at[i],
-            device_id={"row": other},
-        )
-        for i, other in enumerate((up, down))
-    ]
-    for copy in halos:
-        copy.start()
-
     perm = cell_major()
     loads[0].wait()
     own = dot(perm, tok[...]).astype(bf16)
+    mine[...] = own
+    pl.semaphore_wait(barrier, 2 + GROUP - 1 + n_groups - 1)
+
+    pieces = (pl.ds(0, PIECE), pl.ds(PIECE, T - PIECE))
+    halos = [
+        [
+            pltpu.make_async_remote_copy(
+                src_ref=mine.at[piece],
+                dst_ref=halo.at[i, piece],
+                send_sem=halo_send.at[i, w],
+                recv_sem=halo_recv.at[i, w],
+                device_id={"row": other},
+            )
+            for i, other in enumerate((up, down))
+        ]
+        for w, piece in enumerate(pieces)
+    ]
+    for copy in halos[0] + halos[1]:
+        copy.start()
+
     loads[1].wait()
     gs = dot(own, gatew[...], NT).astype(bf16).astype(f32)
     gate[...] = gs[:, :INNER]
@@ -182,24 +201,51 @@
     for load in loads[3:5]:
         load.wait()
 
-    for copy in halos:
-        copy.wait()
-    low = jnp.where(row > 0, dot(perm, halo[0]), 0.0).astype(bf16)
-    high = jnp.where(row < n_row - 1, dot(perm, halo[1]), 0.0).astype(bf16)
-    sides = jnp.concatenate([low, high], axis=0)
-
-    def activated(start, size):
+    def activated(wave, sides, start, size):
         z = dot(sides, mixw[start : start + size, :], NT).astype(bf16).astype(f32)
-        taps = [[taps_ref[i, j : j + 1, start : start + size] for j in range(3)] for i in range(3)]
-        rows = [z[:T], center[:, start : start + size], z[T:]]
-        return convolve(rows, taps, cbias_ref[start : start + size].reshape(1, size))
-
-    def send_all(send, recv, send_sem, recv_sem):
+        n = z.shape[0] // 2
+        cols = slice(start, start + size)
+        new = slice(0, PIECE) if wave == 0 else slice(PIECE, T)
+        side[0, new, cols] = jnp.where(row > 0, z[:n], 0.0)
+        side[1, new, cols] = jnp.where(row < n_row - 1, z[n:], 0.0)
+        taps = [[taps_ref[i, j : j + 1, cols] for j in range(3)] for i in range(3)]
+        rows = [
+            lambda a, b: side[0, a:b, cols],
+            lambda a, b: center[a:b, cols],
+            lambda a, b: side[1, a:b, cols],
+        ]
+        return convolve(wave, rows, taps, cbias_ref[cols].reshape(1, size))
+
+    def send_wave(wave, part):
+        def copy(other):
+            return pltpu.make_async_remote_copy(
+                src_ref=send1.at[part, GW // 2 * wave + other],
+                dst_ref=recv1.at[part, member],
+                send_sem=one_send.at[part],
+                recv_sem=one_recv.at[part],
+                device_id={"tm": group * GROUP + 2 * other + wave},
+            )
+
+        def one(i, c):
+            copy(lax.rem(chip + i, GROUP // 2)).start()
+            return c
+
+        lax.fori_loop(1, GROUP // 2, one, 0)
+
+        @pl.when(core == wave)
+        def _():
+            recv1[part, member] = send1[part, cell]
+
+        @pl.when(core != wave)
+        def _():
+            copy(chip).start()
+
+    def return_all(send, recv, send_sem, recv_sem):
         def one(i, c):
             other = peer(i)
             pltpu.make_async_remote_copy(
                 src_ref=send.at[other],
-                dst_ref=recv.at[member],
+                dst_ref=recv.at[cell],
                 send_sem=send_sem,
                 recv_sem=recv_sem,
                 device_id={"tm": group * GROUP + other},
@@ -207,25 +253,32 @@
             return c
 
         lax.fori_loop(1, GROUP, one, 0)
-        recv[member] = send[member]
+        recv[cell] = send[member]
 
     def wait_all(buf, sem, count=GROUP - 1):
         every = buf.at[pl.ds(0, count)]
         pltpu.make_async_copy(every, every, sem).wait()
 
-    key = activated(INNER, 32)
-    key = jnp.concatenate([key, jnp.zeros((T, 96), f32)], axis=1)
-    extra = jnp.where(lanes(T) < STEP, key, steps)
-    first = activated(0, 384)
-    value[:, :384] = first
-    send1[0] = packets([extra] + [first[:, 128 * j : 128 * (j + 1)] for j in range(3)])
-    send_all(send1.at[0], recv1.at[0], one_send.at[0], one_recv.at[0])
-    second = activated(384, 384)
-    value[:, 384:] = second
-    send1[1] = packets(
-        [second[:, 128 * j : 128 * (j + 1)] for j in range(3)] + [jnp.zeros((T, 128), f32)]
-    )
-    send_all(send1.at[1], recv1.at[1], one_send.at[1], one_recv.at[1])
+    for wave in range(2):
+        for copy in halos[wave]:
+            copy.wait_recv()
+        rows = slice(HALF * wave, HALF * (wave + 1))
+        cells = slice(GW // 2 * wave, GW // 2 * (wave + 1))
+        sides = halo[:, :PIECE] if wave == 0 else halo[:, PIECE:]
+        sides = sides.reshape(-1, D)
+        key = activated(wave, sides, INNER, 32)
+        key = jnp.concatenate([key, jnp.zeros((HALF, 96), f32)], axis=1)
+        extra = jnp.where(lanes(HALF) < STEP, key, steps[rows])
+        act = activated(wave, sides, 0, 384)
+        value[rows, :384] = act
+        send1[0, cells] = packets([extra] + [act[:, 128 * j : 128 * (j + 1)] for j in range(3)])
+        send_wave(wave, 0)
+        act = activated(wave, sides, 384, 384)
+        value[rows, 384:] = act
+        send1[1, cells] = packets(
+            [act[:, 128 * j : 128 * (j + 1)] for j in range(3)] + [jnp.zeros((HALF, 128), f32)]
+        )
+        send_wave(wave, 1)
 
     lane = lanes(1)
     bias_lane = jnp.zeros((1, 128), f32)
@@ -310,7 +363,7 @@
 
     def send_back(third, tiles):
         send2[third] = packets(tiles)
-        send_all(send2.at[third], recv2.at[third], two_send.at[third], two_recv.at[third])
+        return_all(send2.at[third], recv2.at[third], two_send.at[third], two_recv.at[third])
 
     def result(carried, j):
         k = j % 3
@@ -343,6 +396,8 @@
     loads[6].wait()
     o_ref[...] = (tok[...].astype(f32) + dot(normed, outw[...])).astype(bf16)
 
+    for copy in halos[0] + halos[1]:
+        copy.wait_send()
     for part in range(2):
         wait_all(send1.at[part], one_send.at[part])
         wait_all(state_in.at[part], state_send.at[part], n_groups - 1)
@@ -365,14 +420,14 @@
     norm_gain,
     out_weight,
 ):
-    hbm = pl.BlockSpec(memory_space=pl.ANY)
+    hbm = pl.BlockSpec(memory_space=pltpu.HBM)
     vmem = pl.BlockSpec(memory_space=pltpu.VMEM)
     smem = pl.BlockSpec(memory_space=pltpu.SMEM)
     dma = pltpu.SemaphoreType.DMA
     n_groups = n_tm // GROUP
     out = pl.pallas_call(
         functools.partial(kernel, n_tm, n_row),
-        out_shape=jax.ShapeDtypeStruct((T, D), bf16),
+        out_shape=pltpu.VMEM((T, D), bf16),
         in_specs=[hbm] * 7 + [smem] * 3,
         out_specs=vmem,
         scratch_shapes=[
@@ -384,7 +439,9 @@
             pltpu.VMEM((3, 3, CONV_CH), f32),
             pltpu.VMEM((CONV_CH,), f32),
             pltpu.VMEM((INNER,), f32),
+            pltpu.VMEM((T, D), bf16),
             pltpu.VMEM((T, CONV_CH), f32),
+            pltpu.VMEM((2, T, CONV_CH), f32),
             pltpu.VMEM((T, INNER), f32),
             pltpu.VMEM((T, INNER), f32),
             pltpu.VMEM((2, GROUP, 4 * F, 128), bf16),
@@ -396,8 +453,8 @@
             pltpu.VMEM((3, GROUP, 2 * F, 128), bf16),
             pltpu.VMEM((3, GROUP, 2 * F, 128), bf16),
             dma((7,)),
-            dma((2,)),
-            dma((2,)),
+            dma((2, 2)),
+            dma((2, 2)),
             dma((2,)),
             dma((2,)),
             dma((3,)),
@@ -406,7 +463,7 @@
             dma((3,)),
         ],
         compiler_params=pltpu.CompilerParams(
-            collective_id=0, has_side_effects=True, vmem_limit_bytes=60 * 1024 * 1024
+            collective_id=0, has_side_effects=True, vmem_limit_bytes=56 * 1024 * 1024
         ),
     )(
         depth_tokens.reshape(T, D),

time: 45.2 us -> 41.4 us (0.916)
  Pallas kernels: 43.5 us -> 40.6 us
  local copies, waits for them, and re-layouts: 1.62 us -> 0.68 us
    pallas_call x1, Pallas kernels: 43.5 us -> 40.6 us  [per_device(): pl.pallas_call(functools.partial(kernel, n_tm, n_row), out_shape=pltpu.VM...]
    unnamed x1, local copies, waits for them, and re-layouts: 1.62 us -> 0.68 us
where the time goes in v3:
time: 41.4 us; the launch traced here: 41.3 us
  Pallas kernels  40.6 us (98%)
  local copies, waits for them, and re-layouts  0.68 us (2%)
    pallas_call x1, Pallas kernels, per_device(): pl.pallas_call(functools.partial(kernel, n_tm, n_row), out_shape=pltpu.VM...  40.6 us

profile of v3, /device:TPU:1, one launch (start us, length us, event | category | flops | bytes accessed | tf_op | source)
XLA Modules:
  0.0 41.3 jit_solution(11589928933200166318)
XLA Ops:
  0.0 40.6 %shard_map.100 = bf16[128,768]{1,0:T(8,128)(2,1)S(1)} custom-call(bf16[128,768]{1,0:T(8,128)(2,1)} %bitcast.9, bf16[800,768]{1,0:T(8,128)(2,1)} %bitcast.7, bf16[780,768]{1,0:T(8,128)(2,1)} %bitcast.8, bf16[768,768]{1,0:T(8,128)(2,1)} %out_hbm.1, f32[3,3,800]{2,1,0:T(4,128)} %taps_hbm.1, f32[800]{0:T(1024)} %cbias_hbm.1, f32[768]{0:T(1024)} %gain_hbm.1, ...), custom_call_target="tpu_custom_call" | custom-call | tf_op jit(solution)/shard_map/pallas_call | solution.py:428
  40.6 0.7 %copy.13 = bf16[8,1,16,768]{3,2,1,0:T(8,128)(2,1)} copy(bf16[8,1,16,768]{3,2,1,0:T(8,128)(2,1)S(1)} %bitcast.6) | data formatting | bytes 393216

commit v4 on v3

--- a/solution.py
+++ b/solution.py
@@ -17,8 +17,10 @@
 T = F * GW
 GROUP = 16
 SPAN = 128
-HALF = 64
-PIECE = 80
+WAVES = 4
+CELLS = GW // WAVES
+ROWS = CELLS * F
+PIECES = (0, 48, 80, 112, 128)
 KEY = 0
 STEP = 32
 
@@ -57,7 +59,7 @@
 
 
 def convolve(wave, rows, taps, bias):
-    low, high = HALF * wave, HALF * (wave + 1)
+    low, high = ROWS * wave, ROWS * (wave + 1)
 
     def part(j, start, stop):
         z = [r(start, stop) for r in rows]
@@ -66,10 +68,12 @@
     edge = jnp.zeros((F, bias.shape[1]), f32)
     if wave == 0:
         left = jnp.concatenate([edge, part(0, low, high - F)], axis=0)
-        right = part(2, low + F, high + F)
     else:
         left = part(0, low - F, high - F)
+    if wave == WAVES - 1:
         right = jnp.concatenate([part(2, low + F, high), edge], axis=0)
+    else:
+        right = part(2, low + F, high + F)
     return silu(part(1, low, high) + left + right + bias)
 
 
@@ -108,8 +112,12 @@
     side,
     value,
     gate,
-    send1,
-    recv1,
+    send_e,
+    recv_e,
+    send_a,
+    recv_a,
+    send_b,
+    recv_b,
     state_out,
     state_in,
     fade_out,
@@ -135,7 +143,8 @@
     member = lax.rem(me, GROUP)
     chip = member // 2
     core = lax.rem(member, 2)
-    cell = core * (GW // 2) + chip
+    my_wave = 2 * core + lax.rem(chip, 2)
+    cell = CELLS * my_wave + chip // 2
 
     def peer(i):
         return lax.rem(member + i, GROUP)
@@ -144,11 +153,9 @@
     for other in (up, down):
         pl.semaphore_signal(barrier, inc=1, device_id={"row": other})
 
-    def greet(i, c):
-        pl.semaphore_signal(barrier, inc=1, device_id={"tm": group * GROUP + peer(i)})
-        return c
-
-    lax.fori_loop(1, GROUP, greet, 0)
+    for i in range(1, GROUP):
+        far = GROUP // 2 + (i // 2 if i % 2 else -(i // 2))
+        pl.semaphore_signal(barrier, inc=1, device_id={"tm": group * GROUP + peer(far)})
     for i in range(1, n_groups):
         pl.semaphore_signal(barrier, inc=1, device_id={"tm": lax.rem(me + GROUP * i, n_tm)})
 
@@ -174,7 +181,7 @@
     mine[...] = own
     pl.semaphore_wait(barrier, 2 + GROUP - 1 + n_groups - 1)
 
-    pieces = (pl.ds(0, PIECE), pl.ds(PIECE, T - PIECE))
+    pieces = [pl.ds(a, b - a) for a, b in zip(PIECES[:-1], PIECES[1:])]
     halos = [
         [
             pltpu.make_async_remote_copy(
@@ -188,8 +195,9 @@
         ]
         for w, piece in enumerate(pieces)
     ]
-    for copy in halos[0] + halos[1]:
-        copy.start()
+    for pair in halos:
+        for copy in pair:
+            copy.start()
 
     loads[1].wait()
     gs = dot(own, gatew[...], NT).astype(bf16).astype(f32)
@@ -205,7 +213,7 @@
         z = dot(sides, mixw[start : start + size, :], NT).astype(bf16).astype(f32)
         n = z.shape[0] // 2
         cols = slice(start, start + size)
-        new = slice(0, PIECE) if wave == 0 else slice(PIECE, T)
+        new = slice(PIECES[wave], PIECES[wave + 1])
         side[0, new, cols] = jnp.where(row > 0, z[:n], 0.0)
         side[1, new, cols] = jnp.where(row < n_row - 1, z[n:], 0.0)
         taps = [[taps_ref[i, j : j + 1, cols] for j in range(3)] for i in range(3)]
@@ -216,29 +224,30 @@
         ]
         return convolve(wave, rows, taps, cbias_ref[cols].reshape(1, size))
 
-    def send_wave(wave, part):
-        def copy(other):
+    def send_wave(wave, send, recv, which):
+        def target(k):
+            return 4 * k + 2 * (wave % 2) + wave // 2
+
+        def copy(k):
             return pltpu.make_async_remote_copy(
-                src_ref=send1.at[part, GW // 2 * wave + other],
-                dst_ref=recv1.at[part, member],
-                send_sem=one_send.at[part],
-                recv_sem=one_recv.at[part],
-                device_id={"tm": group * GROUP + 2 * other + wave},
+                src_ref=send.at[CELLS * wave + k],
+                dst_ref=recv.at[member],
+                send_sem=one_send.at[which],
+                recv_sem=one_recv.at[which],
+                device_id={"tm": group * GROUP + target(k)},
             )
 
-        def one(i, c):
-            copy(lax.rem(chip + i, GROUP // 2)).start()
-            return c
-
-        lax.fori_loop(1, GROUP // 2, one, 0)
-
-        @pl.when(core == wave)
+        own_k = chip // 2
+        for i in range(1, CELLS):
+            copy(lax.rem(own_k + i, CELLS)).start()
+
+        @pl.when(my_wave == wave)
         def _():
-            recv1[part, member] = send1[part, cell]
-
-        @pl.when(core != wave)
+            recv[member] = send[cell]
+
+        @pl.when(my_wave != wave)
         def _():
-            copy(chip).start()
+            copy(own_k).start()
 
     def return_all(send, recv, send_sem, recv_sem):
         def one(i, c):
@@ -259,26 +268,28 @@
         every = buf.at[pl.ds(0, count)]
         pltpu.make_async_copy(every, every, sem).wait()
 
-    for wave in range(2):
+    for wave in range(WAVES):
         for copy in halos[wave]:
             copy.wait_recv()
-        rows = slice(HALF * wave, HALF * (wave + 1))
-        cells = slice(GW // 2 * wave, GW // 2 * (wave + 1))
-        sides = halo[:, :PIECE] if wave == 0 else halo[:, PIECE:]
-        sides = sides.reshape(-1, D)
+        rows = slice(ROWS * wave, ROWS * (wave + 1))
+        cells = slice(CELLS * wave, CELLS * (wave + 1))
+        sides = halo[:, PIECES[wave] : PIECES[wave + 1]].reshape(-1, D)
         key = activated(wave, sides, INNER, 32)
-        key = jnp.concatenate([key, jnp.zeros((HALF, 96), f32)], axis=1)
-        extra = jnp.where(lanes(HALF) < STEP, key, steps[rows])
-        act = activated(wave, sides, 0, 384)
-        value[rows, :384] = act
-        send1[0, cells] = packets([extra] + [act[:, 128 * j : 128 * (j + 1)] for j in range(3)])
-        send_wave(wave, 0)
-        act = activated(wave, sides, 384, 384)
-        value[rows, 384:] = act
-        send1[1, cells] = packets(
-            [act[:, 128 * j : 128 * (j + 1)] for j in range(3)] + [jnp.zeros((HALF, 128), f32)]
-        )
-        send_wave(wave, 1)
+        key = jnp.concatenate([key, jnp.zeros((ROWS, 96), f32)], axis=1)
+        extra = jnp.where(lanes(ROWS) < STEP, key, steps[rows])
+        late = pltpu.roll(extra, 64, 1).reshape(CELLS, F, 128)[:, F // 2 :]
+        early = extra.reshape(CELLS, F, 128)[:, : F // 2]
+        front = lax.broadcasted_iota(jnp.int32, early.shape, 2) < 64
+        send_e[cells] = jnp.where(front, early, late)
+        send_wave(wave, send_e, recv_e, 0)
+        act = activated(wave, sides, 0, 512)
+        value[rows, :512] = act
+        send_a[cells] = packets([act[:, 128 * j : 128 * (j + 1)] for j in range(4)])
+        send_wave(wave, send_a, recv_a, 1)
+        act = activated(wave, sides, 512, 256)
+        value[rows, 512:] = act
+        send_b[cells] = packets([act[:, 128 * j : 128 * (j + 1)] for j in range(2)])
+        send_wave(wave, send_b, recv_b, 2)
 
     lane = lanes(1)
     bias_lane = jnp.zeros((1, 128), f32)
@@ -297,20 +308,25 @@
     def both(a, j):
         return jnp.where(half[: a.shape[0]], col(a, 2 * j), col(a, 2 * j + 1))
 
+    blocks = (pl.ds(0, 2), pl.ds(2, 1))
+
     def send_state(part):
         for i in range(1, n_groups):
             pltpu.make_async_remote_copy(
-                src_ref=state_out.at[part],
-                dst_ref=state_in.at[part, i - 1],
+                src_ref=state_out.at[blocks[part]],
+                dst_ref=state_in.at[i - 1, blocks[part]],
                 send_sem=state_send.at[part],
                 recv_sem=state_recv.at[part],
                 device_id={"tm": lax.rem(me + GROUP * i, n_tm)},
             ).start()
 
-    wait_all(recv1.at[0], one_recv.at[0])
-    block = recv1[0].astype(f32)
-    extra = unpack(block, 0)
-    x = [unpack(block, j) for j in range(1, 4)]
+    def wait_state(part, sem):
+        every = state_in.at[pl.ds(0, n_groups - 1), blocks[part]]
+        pltpu.make_async_copy(every, every, sem).wait()
+
+    wait_all(recv_e, one_recv.at[0])
+    early = recv_e[...]
+    extra = jnp.concatenate([early, pltpu.roll(early, 64, 2)], axis=1).reshape(SPAN, 128)
     step = softplus(extra + bias_lane)
     tri = jnp.where(past, 1.0, 0.0).astype(f32)
     cum = dot(tri, -step * rate_lane, precision=lax.Precision.HIGHEST)
@@ -327,14 +343,21 @@
     weight = jnp.exp(end - cum) * step
     write = extra[:, :NSTATE].astype(bf16)
     read = extra[:, NSTATE : 2 * NSTATE].astype(bf16)
-    scaled = jnp.concatenate([x[j] * both(weight, j) for j in range(3)], axis=1).astype(bf16)
-    state_out[0] = dot(write, scaled, TN).astype(bf16)
+
+    def local_state(j, x):
+        scaled = jnp.concatenate([x[k] * both(weight, j + k) for k in range(2)], axis=1)
+        state_out[j // 2] = dot(write, scaled.astype(bf16), TN).astype(bf16)
+
+    wait_all(recv_a, one_recv.at[1])
+    block = recv_a[...].astype(f32)
+    x = [unpack(block, j) for j in range(4)]
+    local_state(0, x[:2])
+    local_state(2, x[2:])
     send_state(0)
-    wait_all(recv1.at[1], one_recv.at[1])
-    block = recv1[1].astype(f32)
-    x = x + [unpack(block, j) for j in range(3)]
-    scaled = jnp.concatenate([x[j] * both(weight, j) for j in range(3, 6)], axis=1).astype(bf16)
-    state_out[1] = dot(write, scaled, TN).astype(bf16)
+    wait_all(recv_b, one_recv.at[2])
+    block = recv_b[...].astype(f32)
+    x = x + [unpack(block, j) for j in range(2)]
+    local_state(4, x[4:])
     send_state(1)
 
     late = jnp.transpose(jnp.log(step) - cum)
@@ -353,28 +376,29 @@
     wait_all(fade_in, state_recv.at[2], n_groups - 1)
     fades = [jnp.exp(fade_in[i][:1]) for i in range(n_groups - 1)]
 
-    def arrived(part):
-        wait_all(state_in.at[part], state_recv.at[part], n_groups - 1)
-        total = jnp.zeros((NSTATE, 384), f32)
+    def carried(block):
+        total = jnp.zeros((NSTATE, 256), f32)
         for i in range(n_groups - 2, -1, -1):
-            fade = jnp.concatenate([both(fades[i], 3 * part + j) for j in range(3)], axis=1)
-            total = jnp.where(group > i, total * fade + state_in[part, i].astype(f32), 0.0)
+            fade = jnp.concatenate([both(fades[i], 2 * block + k) for k in range(2)], axis=1)
+            total = jnp.where(group > i, total * fade + state_in[i, block].astype(f32), 0.0)
         return dot(read, total.astype(bf16))
 
     def send_back(third, tiles):
         send2[third] = packets(tiles)
         return_all(send2.at[third], recv2.at[third], two_send.at[third], two_recv.at[third])
 
-    def result(carried, j):
-        k = j % 3
-        return inner[j] + both(reach, j) * carried[:, 128 * k : 128 * (k + 1)]
-
-    carried = arrived(0)
-    send_back(0, [result(carried, 0), result(carried, 1)])
-    third = result(carried, 2)
-    carried = arrived(1)
-    send_back(1, [third, result(carried, 3)])
-    send_back(2, [result(carried, 4), result(carried, 5)])
+    def results(block):
+        rest = carried(block)
+        return [
+            inner[2 * block + k] + both(reach, 2 * block + k) * rest[:, 128 * k : 128 * (k + 1)]
+            for k in range(2)
+        ]
+
+    wait_state(0, state_recv.at[0])
+    send_back(0, results(0))
+    send_back(1, results(1))
+    wait_state(1, state_recv.at[1])
+    send_back(2, results(2))
 
     loads[5].wait()
     lane = lanes(1)
@@ -396,11 +420,13 @@
     loads[6].wait()
     o_ref[...] = (tok[...].astype(f32) + dot(normed, outw[...])).astype(bf16)
 
-    for copy in halos[0] + halos[1]:
-        copy.wait_send()
+    for pair in halos:
+        for copy in pair:
+            copy.wait_send()
+    for i, buf in enumerate((send_e, send_a, send_b)):
+        wait_all(buf, one_send.at[i])
     for part in range(2):
-        wait_all(send1.at[part], one_send.at[part])
-        wait_all(state_in.at[part], state_send.at[part], n_groups - 1)
+        wait_state(part, state_send.at[part])
     wait_all(fade_in, state_send.at[2], n_groups - 1)
     for third in range(3):
         wait_all(send2.at[third], two_send.at[third])
@@ -444,19 +470,23 @@
             pltpu.VMEM((2, T, CONV_CH), f32),
             pltpu.VMEM((T, INNER), f32),
             pltpu.VMEM((T, INNER), f32),
-            pltpu.VMEM((2, GROUP, 4 * F, 128), bf16),
-            pltpu.VMEM((2, GROUP, 4 * F, 128), bf16),
-            pltpu.VMEM((2, NSTATE, 384), bf16),
-            pltpu.VMEM((2, n_groups - 1, NSTATE, 384), bf16),
+            pltpu.VMEM((GROUP, F // 2, 128), f32),
+            pltpu.VMEM((GROUP, F // 2, 128), f32),
+            pltpu.VMEM((GROUP, 4 * F, 128), bf16),
+            pltpu.VMEM((GROUP, 4 * F, 128), bf16),
+            pltpu.VMEM((GROUP, 2 * F, 128), bf16),
+            pltpu.VMEM((GROUP, 2 * F, 128), bf16),
+            pltpu.VMEM((3, NSTATE, 256), bf16),
+            pltpu.VMEM((n_groups - 1, 3, NSTATE, 256), bf16),
             pltpu.VMEM((8, 128), f32),
             pltpu.VMEM((n_groups - 1, 8, 128), f32),
             pltpu.VMEM((3, GROUP, 2 * F, 128), bf16),
             pltpu.VMEM((3, GROUP, 2 * F, 128), bf16),
             dma((7,)),
-            dma((2, 2)),
-            dma((2, 2)),
-            dma((2,)),
-            dma((2,)),
+            dma((2, WAVES)),
+            dma((2, WAVES)),
+            dma((3,)),
+            dma((3,)),
             dma((3,)),
             dma((3,)),
             dma((3,)),

time: 41.4 us -> 40.6 us (0.981)
  Pallas kernels: 40.6 us -> 39.7 us
    pallas_call x1, Pallas kernels: 40.6 us -> 39.7 us  [per_device(): pl.pallas_call(functools.partial(kernel, n_tm, n_row), out_shape=pltpu.VM...]
where the time goes in v4:
time: 40.6 us; the launch traced here: 40.4 us
  Pallas kernels  39.7 us (98%)
  local copies, waits for them, and re-layouts  0.68 us (2%)
    pallas_call x1, Pallas kernels, per_device(): pl.pallas_call(functools.partial(kernel, n_tm, n_row), out_shape=pltpu.VM...  39.7 us

profile of v4, /device:TPU:1, one launch (start us, length us, event | category | flops | bytes accessed | tf_op | source)
XLA Modules:
  0.0 40.4 jit_solution(1541750355337545488)
XLA Ops:
  0.0 39.7 %shard_map.100 = bf16[128,768]{1,0:T(8,128)(2,1)S(1)} custom-call(bf16[128,768]{1,0:T(8,128)(2,1)} %bitcast.9, bf16[800,768]{1,0:T(8,128)(2,1)} %bitcast.7, bf16[780,768]{1,0:T(8,128)(2,1)} %bitcast.8, bf16[768,768]{1,0:T(8,128)(2,1)} %out_hbm.1, f32[3,3,800]{2,1,0:T(4,128)} %taps_hbm.1, f32[800]{0:T(1024)} %cbias_hbm.1, f32[768]{0:T(1024)} %gain_hbm.1, ...), custom_call_target="tpu_custom_call" | custom-call | tf_op jit(solution)/shard_map/pallas_call | solution.py:454
  39.8 0.7 %copy.13 = bf16[8,1,16,768]{3,2,1,0:T(8,128)(2,1)} copy(bf16[8,1,16,768]{3,2,1,0:T(8,128)(2,1)S(1)} %bitcast.6) | data formatting | bytes 393216

commit v5 on v4

--- a/solution.py
+++ b/solution.py
@@ -124,6 +124,7 @@
     fade_in,
     send2,
     recv2,
+    ready,
     load_sem,
     halo_send,
     halo_recv,
@@ -136,8 +137,6 @@
 ):
     me = lax.axis_index("tm")
     row = lax.axis_index("row")
-    up = lax.rem(row + 1, n_row)
-    down = lax.rem(row + n_row - 1, n_row)
     n_groups = n_tm // GROUP
     group = me // GROUP
     member = lax.rem(me, GROUP)
@@ -149,15 +148,27 @@
     def peer(i):
         return lax.rem(member + i, GROUP)
 
+    later = [(i, group + i < n_groups, me + GROUP * i) for i in range(1, n_groups)]
+    earlier = [(i, group >= i, me - GROUP * i) for i in range(1, n_groups)]
+    has_down, has_up = row > 0, row < n_row - 1
+    toward = ((has_up, row + 1), (has_down, row - 1))
+    origin = (has_down, has_up)
+
     barrier = pltpu.get_barrier_semaphore()
-    for other in (up, down):
-        pl.semaphore_signal(barrier, inc=1, device_id={"row": other})
+    for exists, other in toward:
+
+        @pl.when(exists)
+        def _():
+            pl.semaphore_signal(barrier, inc=1, device_id={"row": other})
 
     for i in range(1, GROUP):
         far = GROUP // 2 + (i // 2 if i % 2 else -(i // 2))
         pl.semaphore_signal(barrier, inc=1, device_id={"tm": group * GROUP + peer(far)})
-    for i in range(1, n_groups):
-        pl.semaphore_signal(barrier, inc=1, device_id={"tm": lax.rem(me + GROUP * i, n_tm)})
+    for i, exists, other in later:
+
+        @pl.when(exists)
+        def _():
+            pl.semaphore_signal(barrier, inc=1, device_id={"tm": other})
 
     loads = [
         pltpu.make_async_copy(src, dst, load_sem.at[i])
@@ -179,7 +190,14 @@
     loads[0].wait()
     own = dot(perm, tok[...]).astype(bf16)
     mine[...] = own
-    pl.semaphore_wait(barrier, 2 + GROUP - 1 + n_groups - 1)
+    neighbours = jnp.minimum(row, 1) + jnp.minimum(n_row - 1 - row, 1)
+    pl.semaphore_wait(barrier, GROUP - 1 + group + neighbours)
+    for i, exists, other in earlier:
+
+        @pl.when(exists)
+        def _():
+            pl.semaphore_signal(ready.at[i - 1], inc=1, device_id={"tm": other})
+
 
     pieces = [pl.ds(a, b - a) for a, b in zip(PIECES[:-1], PIECES[1:])]
     halos = [
@@ -191,13 +209,13 @@
                 recv_sem=halo_recv.at[i, w],
                 device_id={"row": other},
             )
-            for i, other in enumerate((up, down))
+            for i, (_, other) in enumerate(toward)
         ]
         for w, piece in enumerate(pieces)
     ]
     for pair in halos:
-        for copy in pair:
-            copy.start()
+        for (exists, _), copy in zip(toward, pair):
+            pl.when(exists)(copy.start)
 
     loads[1].wait()
     gs = dot(own, gatew[...], NT).astype(bf16).astype(f32)
@@ -214,8 +232,8 @@
         n = z.shape[0] // 2
         cols = slice(start, start + size)
         new = slice(PIECES[wave], PIECES[wave + 1])
-        side[0, new, cols] = jnp.where(row > 0, z[:n], 0.0)
-        side[1, new, cols] = jnp.where(row < n_row - 1, z[n:], 0.0)
+        side[0, new, cols] = jnp.where(has_down, z[:n], 0.0)
+        side[1, new, cols] = jnp.where(has_up, z[n:], 0.0)
         taps = [[taps_ref[i, j : j + 1, cols] for j in range(3)] for i in range(3)]
         rows = [
             lambda a, b: side[0, a:b, cols],
@@ -269,8 +287,8 @@
         pltpu.make_async_copy(every, every, sem).wait()
 
     for wave in range(WAVES):
-        for copy in halos[wave]:
-            copy.wait_recv()
+        for exists, copy in zip(origin, halos[wave]):
+            pl.when(exists)(copy.wait_recv)
         rows = slice(ROWS * wave, ROWS * (wave + 1))
         cells = slice(CELLS * wave, CELLS * (wave + 1))
         sides = halo[:, PIECES[wave] : PIECES[wave + 1]].reshape(-1, D)
@@ -310,19 +328,26 @@
 
     blocks = (pl.ds(0, 2), pl.ds(2, 1))
 
+    def state_copy(part, i, other):
+        if part == 2:
+            src, dst = fade_out, fade_in.at[i - 1]
+        else:
+            src, dst = state_out.at[blocks[part]], state_in.at[i - 1, blocks[part]]
+        return pltpu.make_async_remote_copy(
+            src_ref=src,
+            dst_ref=dst,
+            send_sem=state_send.at[part, i - 1],
+            recv_sem=state_recv.at[part, i - 1],
+            device_id={"tm": other},
+        )
+
     def send_state(part):
-        for i in range(1, n_groups):
-            pltpu.make_async_remote_copy(
-                src_ref=state_out.at[blocks[part]],
-                dst_ref=state_in.at[i - 1, blocks[part]],
-                send_sem=state_send.at[part],
-                recv_sem=state_recv.at[part],
-                device_id={"tm": lax.rem(me + GROUP * i, n_tm)},
-            ).start()
-
-    def wait_state(part, sem):
-        every = state_in.at[pl.ds(0, n_groups - 1), blocks[part]]
-        pltpu.make_async_copy(every, every, sem).wait()
+        for i, exists, other in later:
+            pl.when(exists)(state_copy(part, i, other).start)
+
+    def wait_state(part):
+        for i, exists, other in earlier:
+            pl.when(exists)(state_copy(part, i, other).wait_recv)
 
     wait_all(recv_e, one_recv.at[0])
     early = recv_e[...]
@@ -332,14 +357,13 @@
     cum = dot(tri, -step * rate_lane, precision=lax.Precision.HIGHEST)
     end = cum[SPAN - 1 :, :]
     fade_out[...] = jnp.broadcast_to(end, (8, 128))
-    for i in range(1, n_groups):
-        pltpu.make_async_remote_copy(
-            src_ref=fade_out,
-            dst_ref=fade_in.at[i - 1],
-            send_sem=state_send.at[2],
-            recv_sem=state_recv.at[2],
-            device_id={"tm": lax.rem(me + GROUP * i, n_tm)},
-        ).start()
+    for i, exists, other in later:
+
+        @pl.when(exists)
+        def _():
+            pl.semaphore_wait(ready.at[i - 1], 1)
+
+    send_state(2)
     weight = jnp.exp(end - cum) * step
     write = extra[:, :NSTATE].astype(bf16)
     read = extra[:, NSTATE : 2 * NSTATE].astype(bf16)
@@ -373,7 +397,7 @@
             part.append(dot(m.astype(bf16), xb))
         inner.append(jnp.where(half, part[0], part[1]))
 
-    wait_all(fade_in, state_recv.at[2], n_groups - 1)
+    wait_state(2)
     fades = [jnp.exp(fade_in[i][:1]) for i in range(n_groups - 1)]
 
     def carried(block):
@@ -394,10 +418,10 @@
             for k in range(2)
         ]
 
-    wait_state(0, state_recv.at[0])
+    wait_state(0)
     send_back(0, results(0))
     send_back(1, results(1))
-    wait_state(1, state_recv.at[1])
+    wait_state(1)
     send_back(2, results(2))
 
     loads[5].wait()
@@ -421,13 +445,13 @@
     o_ref[...] = (tok[...].astype(f32) + dot(normed, outw[...])).astype(bf16)
 
     for pair in halos:
-        for copy in pair:
-            copy.wait_send()
+        for (exists, _), copy in zip(toward, pair):
+            pl.when(exists)(copy.wait_send)
     for i, buf in enumerate((send_e, send_a, send_b)):
         wait_all(buf, one_send.at[i])
-    for part in range(2):
-        wait_state(part, state_send.at[part])
-    wait_all(fade_in, state_send.at[2], n_groups - 1)
+    for part in range(3):
+        for i, exists, other in later:
+            pl.when(exists)(state_copy(part, i, other).wait_send)
     for third in range(3):
         wait_all(send2.at[third], two_send.at[third])
 
@@ -482,13 +506,14 @@
             pltpu.VMEM((n_groups - 1, 8, 128), f32),
             pltpu.VMEM((3, GROUP, 2 * F, 128), bf16),
             pltpu.VMEM((3, GROUP, 2 * F, 128), bf16),
+            pltpu.SemaphoreType.REGULAR((n_groups - 1,)),
             dma((7,)),
             dma((2, WAVES)),
             dma((2, WAVES)),
             dma((3,)),
             dma((3,)),
-            dma((3,)),
-            dma((3,)),
+            dma((3, n_groups - 1)),
+            dma((3, n_groups - 1)),
             dma((3,)),
             dma((3,)),
         ],

time: 40.6 us -> 37.3 us (0.919)
  the two profiles are of different devices: /device:TPU:1 before, /device:TPU:31 now
where the time goes in v5:
time: 37.3 us; the launch traced here: 37.2 us
  Pallas kernels  36.5 us (98%)
  local copies, waits for them, and re-layouts  0.68 us (2%)
    pallas_call x1, Pallas kernels, per_device(): pl.pallas_call(functools.partial(kernel, n_tm, n_row), out_shape=pltpu.VM...  36.5 us

profile of v5, /device:TPU:31, one launch (start us, length us, event | category | flops | bytes accessed | tf_op | source)
XLA Modules:
  0.0 37.2 jit_solution(8122836833020500365)
XLA Ops:
  0.0 36.5 %shard_map.100 = bf16[128,768]{1,0:T(8,128)(2,1)S(1)} custom-call(bf16[128,768]{1,0:T(8,128)(2,1)} %bitcast.9, bf16[800,768]{1,0:T(8,128)(2,1)} %bitcast.7, bf16[780,768]{1,0:T(8,128)(2,1)} %bitcast.8, bf16[768,768]{1,0:T(8,128)(2,1)} %out_hbm.1, f32[3,3,800]{2,1,0:T(4,128)} %taps_hbm.1, f32[800]{0:T(1024)} %cbias_hbm.1, f32[768]{0:T(1024)} %gain_hbm.1, ...), custom_call_target="tpu_custom_call" | custom-call | tf_op jit(solution)/shard_map/pallas_call | solution.py:478
  36.5 0.7 %copy.13 = bf16[8,1,16,768]{3,2,1,0:T(8,128)(2,1)} copy(bf16[8,1,16,768]{3,2,1,0:T(8,128)(2,1)S(1)} %bitcast.6) | data formatting | bytes 393216

commit v6 on v5

--- a/solution.py
+++ b/solution.py
@@ -154,22 +154,6 @@
     toward = ((has_up, row + 1), (has_down, row - 1))
     origin = (has_down, has_up)
 
-    barrier = pltpu.get_barrier_semaphore()
-    for exists, other in toward:
-
-        @pl.when(exists)
-        def _():
-            pl.semaphore_signal(barrier, inc=1, device_id={"row": other})
-
-    for i in range(1, GROUP):
-        far = GROUP // 2 + (i // 2 if i % 2 else -(i // 2))
-        pl.semaphore_signal(barrier, inc=1, device_id={"tm": group * GROUP + peer(far)})
-    for i, exists, other in later:
-
-        @pl.when(exists)
-        def _():
-            pl.semaphore_signal(barrier, inc=1, device_id={"tm": other})
-
     loads = [
         pltpu.make_async_copy(src, dst, load_sem.at[i])
         for i, (src, dst) in enumerate(
@@ -184,20 +168,34 @@
             )
         )
     ]
-    for load in loads:
+    loads[0].start()
+
+    barrier = pltpu.get_barrier_semaphore()
+    for exists, other in toward:
+
+        @pl.when(exists)
+        def _():
+            pl.semaphore_signal(barrier, inc=1, device_id={"row": other})
+
+    def greet(i, c):
+        pl.semaphore_signal(barrier, inc=1, device_id={"tm": group * GROUP + i})
+        return c
+
+    lax.fori_loop(member + 1, GROUP, greet, 0)
+    for i, exists, other in later:
+
+        @pl.when(exists)
+        def _():
+            pl.semaphore_signal(barrier, inc=1, device_id={"tm": other})
+
+    for load in loads[1:]:
         load.start()
     perm = cell_major()
     loads[0].wait()
     own = dot(perm, tok[...]).astype(bf16)
     mine[...] = own
     neighbours = jnp.minimum(row, 1) + jnp.minimum(n_row - 1 - row, 1)
-    pl.semaphore_wait(barrier, GROUP - 1 + group + neighbours)
-    for i, exists, other in earlier:
-
-        @pl.when(exists)
-        def _():
-            pl.semaphore_signal(ready.at[i - 1], inc=1, device_id={"tm": other})
-
+    pl.semaphore_wait(barrier, member + group + neighbours)
 
     pieces = [pl.ds(a, b - a) for a, b in zip(PIECES[:-1], PIECES[1:])]
     halos = [
@@ -217,6 +215,17 @@
         for (exists, _), copy in zip(toward, pair):
             pl.when(exists)(copy.start)
 
+    def answer(i, c):
+        pl.semaphore_signal(ready.at[0], inc=1, device_id={"tm": group * GROUP + i})
+        return c
+
+    lax.fori_loop(0, member, answer, 0)
+    for i, exists, other in earlier:
+
+        @pl.when(exists)
+        def _():
+            pl.semaphore_signal(ready.at[i], inc=1, device_id={"tm": other})
+
     loads[1].wait()
     gs = dot(own, gatew[...], NT).astype(bf16).astype(f32)
     gate[...] = gs[:, :INNER]
@@ -285,6 +294,10 @@
     def wait_all(buf, sem, count=GROUP - 1):
         every = buf.at[pl.ds(0, count)]
         pltpu.make_async_copy(every, every, sem).wait()
+
+    @pl.when(member < GROUP - 1)
+    def _():
+        pl.semaphore_wait(ready.at[0], GROUP - 1 - member)
 
     for wave in range(WAVES):
         for exists, copy in zip(origin, halos[wave]):
@@ -361,7 +374,7 @@
 
         @pl.when(exists)
         def _():
-            pl.semaphore_wait(ready.at[i - 1], 1)
+            pl.semaphore_wait(ready.at[i], 1)
 
     send_state(2)
     weight = jnp.exp(end - cum) * step
@@ -506,7 +519,7 @@
             pltpu.VMEM((n_groups - 1, 8, 128), f32),
             pltpu.VMEM((3, GROUP, 2 * F, 128), bf16),
             pltpu.VMEM((3, GROUP, 2 * F, 128), bf16),
-            pltpu.SemaphoreType.REGULAR((n_groups - 1,)),
+            pltpu.SemaphoreType.REGULAR((n_groups,)),
             dma((7,)),
             dma((2, WAVES)),
             dma((2, WAVES)),

time: 37.3 us -> 35.4 us (0.949)
  the two profiles are of different devices: /device:TPU:31 before, /device:TPU:23 now
where the time goes in v6:
time: 35.4 us; the launch traced here: 35.3 us
  Pallas kernels  34.6 us (98%)
  local copies, waits for them, and re-layouts  0.68 us (2%)
    pallas_call x1, Pallas kernels, per_device(): pl.pallas_call(functools.partial(kernel, n_tm, n_row), out_shape=pltpu.VM...  34.6 us

profile of v6, /device:TPU:23, one launch (start us, length us, event | category | flops | bytes accessed | tf_op | source)
XLA Modules:
  0.0 35.3 jit_solution(18131435163144868429)
XLA Ops:
  0.0 34.6 %shard_map.100 = bf16[128,768]{1,0:T(8,128)(2,1)S(1)} custom-call(bf16[128,768]{1,0:T(8,128)(2,1)} %bitcast.9, bf16[800,768]{1,0:T(8,128)(2,1)} %bitcast.7, bf16[780,768]{1,0:T(8,128)(2,1)} %bitcast.8, bf16[768,768]{1,0:T(8,128)(2,1)} %out_hbm.1, f32[3,3,800]{2,1,0:T(4,128)} %taps_hbm.1, f32[800]{0:T(1024)} %cbias_hbm.1, f32[768]{0:T(1024)} %gain_hbm.1, ...), custom_call_target="tpu_custom_call" | custom-call | tf_op jit(solution)/shard_map/pallas_call | solution.py:491
  34.6 0.7 %copy.13 = bf16[8,1,16,768]{3,2,1,0:T(8,128)(2,1)} copy(bf16[8,1,16,768]{3,2,1,0:T(8,128)(2,1)S(1)} %bitcast.6) | data formatting | bytes 393216

commit v7 on v6

--- a/solution.py
+++ b/solution.py
@@ -140,10 +140,8 @@
     n_groups = n_tm // GROUP
     group = me // GROUP
     member = lax.rem(me, GROUP)
-    chip = member // 2
-    core = lax.rem(member, 2)
-    my_wave = 2 * core + lax.rem(chip, 2)
-    cell = CELLS * my_wave + chip // 2
+    cell = member
+    my_wave, own_k = member // CELLS, lax.rem(member, CELLS)
 
     def peer(i):
         return lax.rem(member + i, GROUP)
@@ -216,7 +214,7 @@
             pl.when(exists)(copy.start)
 
     def answer(i, c):
-        pl.semaphore_signal(ready.at[0], inc=1, device_id={"tm": group * GROUP + i})
+        pl.semaphore_signal(ready.at[member], inc=1, device_id={"tm": group * GROUP + i})
         return c
 
     lax.fori_loop(0, member, answer, 0)
@@ -224,7 +222,7 @@
 
         @pl.when(exists)
         def _():
-            pl.semaphore_signal(ready.at[i], inc=1, device_id={"tm": other})
+            pl.semaphore_signal(ready.at[GROUP + i - 1], inc=1, device_id={"tm": other})
 
     loads[1].wait()
     gs = dot(own, gatew[...], NT).astype(bf16).astype(f32)
@@ -252,21 +250,28 @@
         return convolve(wave, rows, taps, cbias_ref[cols].reshape(1, size))
 
     def send_wave(wave, send, recv, which):
-        def target(k):
-            return 4 * k + 2 * (wave % 2) + wave // 2
-
         def copy(k):
+            other = CELLS * wave + k
             return pltpu.make_async_remote_copy(
-                src_ref=send.at[CELLS * wave + k],
+                src_ref=send.at[other],
                 dst_ref=recv.at[member],
                 send_sem=one_send.at[which],
                 recv_sem=one_recv.at[which],
-                device_id={"tm": group * GROUP + target(k)},
+                device_id={"tm": group * GROUP + other},
             )
 
-        own_k = chip // 2
+        def one(k):
+            if which == 0:
+                other = CELLS * wave + k
+
+                @pl.when(other > member)
+                def _():
+                    pl.semaphore_wait(ready.at[other], 1)
+
+            copy(k).start()
+
         for i in range(1, CELLS):
-            copy(lax.rem(own_k + i, CELLS)).start()
+            one(lax.rem(own_k + i, CELLS))
 
         @pl.when(my_wave == wave)
         def _():
@@ -274,11 +279,11 @@
 
         @pl.when(my_wave != wave)
         def _():
-            copy(own_k).start()
+            one(own_k)
 
     def return_all(send, recv, send_sem, recv_sem):
-        def one(i, c):
-            other = peer(i)
+        for i in range(1, GROUP):
+            other = peer(GROUP // 2 + (i // 2 if i % 2 else -(i // 2)))
             pltpu.make_async_remote_copy(
                 src_ref=send.at[other],
                 dst_ref=recv.at[cell],
@@ -286,18 +291,11 @@
                 recv_sem=recv_sem,
                 device_id={"tm": group * GROUP + other},
             ).start()
-            return c
-
-        lax.fori_loop(1, GROUP, one, 0)
         recv[cell] = send[member]
 
     def wait_all(buf, sem, count=GROUP - 1):
         every = buf.at[pl.ds(0, count)]
         pltpu.make_async_copy(every, every, sem).wait()
-
-    @pl.when(member < GROUP - 1)
-    def _():
-        pl.semaphore_wait(ready.at[0], GROUP - 1 - member)
 
     for wave in range(WAVES):
         for exists, copy in zip(origin, halos[wave]):
@@ -374,7 +372,7 @@
 
         @pl.when(exists)
         def _():
-            pl.semaphore_wait(ready.at[i], 1)
+            pl.semaphore_wait(ready.at[GROUP + i - 1], 1)
 
     send_state(2)
     weight = jnp.exp(end - cum) * step
@@ -397,7 +395,7 @@
     local_state(4, x[4:])
     send_state(1)
 
-    late = jnp.transpose(jnp.log(step) - cum)
+    turned = jnp.transpose(jnp.where(half, cum, pltpu.roll(step, 64, 1)))
     reach = jnp.exp(cum)
     pair = dot(read, write, NT)
     inner = []
@@ -405,8 +403,9 @@
         xb = x[j].astype(bf16)
         part = []
         for h in (2 * j, 2 * j + 1):
-            span = col(cum, h) + late[STEP + h : STEP + h + 1, :]
-            m = pair * jnp.exp(jnp.where(past, span, -1e30))
+            at = STEP + h
+            span = jnp.where(past, col(cum, h) - turned[at : at + 1, :], -1e30)
+            m = pair * (jnp.exp(span) * turned[64 + at : 65 + at, :])
             part.append(dot(m.astype(bf16), xb))
         inner.append(jnp.where(half, part[0], part[1]))
 
@@ -519,7 +518,7 @@
             pltpu.VMEM((n_groups - 1, 8, 128), f32),
             pltpu.VMEM((3, GROUP, 2 * F, 128), bf16),
             pltpu.VMEM((3, GROUP, 2 * F, 128), bf16),
-            pltpu.SemaphoreType.REGULAR((n_groups,)),
+            pltpu.SemaphoreType.REGULAR((GROUP + n_groups - 1,)),
             dma((7,)),
             dma((2, WAVES)),
             dma((2, WAVES)),

time: 35.4 us -> 35 us (0.989)
  Pallas kernels: 34.6 us -> 34.2 us
    pallas_call x1, Pallas kernels: 34.6 us -> 34.2 us  [per_device(): pl.pallas_call(functools.partial(kernel, n_tm, n_row), out_shape=pltpu.VM...]
where the time goes in v7:
time: 35 us; the launch traced here: 34.9 us
  Pallas kernels  34.2 us (98%)
  local copies, waits for them, and re-layouts  0.68 us (2%)
    pallas_call x1, Pallas kernels, per_device(): pl.pallas_call(functools.partial(kernel, n_tm, n_row), out_shape=pltpu.VM...  34.2 us

profile of v7, /device:TPU:23, one launch (start us, length us, event | category | flops | bytes accessed | tf_op | source)
XLA Modules:
  0.0 34.9 jit_solution(2664710354265265343)
XLA Ops:
  0.0 34.2 %shard_map.100 = bf16[128,768]{1,0:T(8,128)(2,1)S(1)} custom-call(bf16[128,768]{1,0:T(8,128)(2,1)} %bitcast.9, bf16[800,768]{1,0:T(8,128)(2,1)} %bitcast.7, bf16[780,768]{1,0:T(8,128)(2,1)} %bitcast.8, bf16[768,768]{1,0:T(8,128)(2,1)} %out_hbm.1, f32[3,3,800]{2,1,0:T(4,128)} %taps_hbm.1, f32[800]{0:T(1024)} %cbias_hbm.1, f32[768]{0:T(1024)} %gain_hbm.1, ...), custom_call_target="tpu_custom_call" | custom-call | tf_op jit(solution)/shard_map/pallas_call | solution.py:490
  34.2 0.7 %copy.13 = bf16[8,1,16,768]{3,2,1,0:T(8,128)(2,1)} copy(bf16[8,1,16,768]{3,2,1,0:T(8,128)(2,1)S(1)} %bitcast.6) | data formatting | bytes 393216

commit v8 on v7

--- a/solution.py
+++ b/solution.py
@@ -281,17 +281,18 @@
         def _():
             one(own_k)
 
-    def return_all(send, recv, send_sem, recv_sem):
-        for i in range(1, GROUP):
-            other = peer(GROUP // 2 + (i // 2 if i % 2 else -(i // 2)))
-            pltpu.make_async_remote_copy(
-                src_ref=send.at[other],
-                dst_ref=recv.at[cell],
-                send_sem=send_sem,
-                recv_sem=recv_sem,
-                device_id={"tm": group * GROUP + other},
-            ).start()
-        recv[cell] = send[member]
+    def return_to(third, members):
+        for other in members:
+
+            @pl.when(other != member)
+            def _():
+                pltpu.make_async_remote_copy(
+                    src_ref=send2.at[third, other],
+                    dst_ref=recv2.at[third, cell],
+                    send_sem=two_send.at[third],
+                    recv_sem=two_recv.at[third],
+                    device_id={"tm": group * GROUP + other},
+                ).start()
 
     def wait_all(buf, sem, count=GROUP - 1):
         every = buf.at[pl.ds(0, count)]
@@ -421,7 +422,8 @@
 
     def send_back(third, tiles):
         send2[third] = packets(tiles)
-        return_all(send2.at[third], recv2.at[third], two_send.at[third], two_recv.at[third])
+        return_to(third, range(GROUP // 4))
+        recv2[third, cell] = send2[third, member]
 
     def results(block):
         rest = carried(block)
@@ -435,6 +437,9 @@
     send_back(1, results(1))
     wait_state(1)
     send_back(2, results(2))
+    for quarter in range(1, 4):
+        for third in range(3):
+            return_to(third, range(GROUP // 4 * quarter, GROUP // 4 * (quarter + 1)))
 
     loads[5].wait()
     lane = lanes(1)

time: 35 us -> 34.5 us (0.986)
  Pallas kernels: 34.2 us -> 33.7 us
    pallas_call x1, Pallas kernels: 34.2 us -> 33.7 us  [per_device(): pl.pallas_call(functools.partial(kernel, n_tm, n_row), out_shape=pltpu.VM...]
where the time goes in v8:
time: 34.5 us; the launch traced here: 34.4 us
  Pallas kernels  33.7 us (98%)
  local copies, waits for them, and re-layouts  0.68 us (2%)
    pallas_call x1, Pallas kernels, per_device(): pl.pallas_call(functools.partial(kernel, n_tm, n_row), out_shape=pltpu.VM...  33.7 us

profile of v8, /device:TPU:23, one launch (start us, length us, event | category | flops | bytes accessed | tf_op | source)
XLA Modules:
  0.0 34.4 jit_solution(4645353551935123658)
XLA Ops:
  0.0 33.7 %shard_map.100 = bf16[128,768]{1,0:T(8,128)(2,1)S(1)} custom-call(bf16[128,768]{1,0:T(8,128)(2,1)} %bitcast.9, bf16[800,768]{1,0:T(8,128)(2,1)} %bitcast.7, bf16[780,768]{1,0:T(8,128)(2,1)} %bitcast.8, bf16[768,768]{1,0:T(8,128)(2,1)} %out_hbm.1, f32[3,3,800]{2,1,0:T(4,128)} %taps_hbm.1, f32[800]{0:T(1024)} %cbias_hbm.1, f32[768]{0:T(1024)} %gain_hbm.1, ...), custom_call_target="tpu_custom_call" | custom-call | tf_op jit(solution)/shard_map/pallas_call | solution.py:495
  33.7 0.7 %copy.13 = bf16[8,1,16,768]{3,2,1,0:T(8,128)(2,1)} copy(bf16[8,1,16,768]{3,2,1,0:T(8,128)(2,1)S(1)} %bitcast.6) | data formatting | bytes 393216

commit v9 on v8

--- a/solution.py
+++ b/solution.py
@@ -354,7 +354,7 @@
         )
 
     def send_state(part):
-        for i, exists, other in later:
+        for i, exists, other in later[1:] + later[:1]:
             pl.when(exists)(state_copy(part, i, other).start)
 
     def wait_state(part):

time: 34.5 us -> 34.5 us (level)
  no operation moved by 1% of the time
where the time goes in v9:
time: 34.5 us; the launch traced here: 34.4 us
  Pallas kernels  33.7 us (98%)
  local copies, waits for them, and re-layouts  0.68 us (2%)
    pallas_call x1, Pallas kernels, per_device(): pl.pallas_call(functools.partial(kernel, n_tm, n_row), out_shape=pltpu.VM...  33.7 us

profile of v9, /device:TPU:23, one launch (start us, length us, event | category | flops | bytes accessed | tf_op | source)
XLA Modules:
  0.0 34.4 jit_solution(7751228833443576128)
XLA Ops:
  0.0 33.7 %shard_map.100 = bf16[128,768]{1,0:T(8,128)(2,1)S(1)} custom-call(bf16[128,768]{1,0:T(8,128)(2,1)} %bitcast.9, bf16[800,768]{1,0:T(8,128)(2,1)} %bitcast.7, bf16[780,768]{1,0:T(8,128)(2,1)} %bitcast.8, bf16[768,768]{1,0:T(8,128)(2,1)} %out_hbm.1, f32[3,3,800]{2,1,0:T(4,128)} %taps_hbm.1, f32[800]{0:T(1024)} %cbias_hbm.1, f32[768]{0:T(1024)} %gain_hbm.1, ...), custom_call_target="tpu_custom_call" | custom-call | tf_op jit(solution)/shard_map/pallas_call | solution.py:495
  33.7 0.7 %copy.13 = bf16[8,1,16,768]{3,2,1,0:T(8,128)(2,1)} copy(bf16[8,1,16,768]{3,2,1,0:T(8,128)(2,1)S(1)} %bitcast.6) | data formatting | bytes 393216
